TPU v7x, 512 devices: a whole 4x4x16 slice. The times are simulated.
512 devices in a mesh: fsdp: 64 (over z, x), tensor: 8 (over y, core).
Axes of the slice: x: 4, y: 4, z: 16, core: 2. Of those that a mesh axis runs over, the one named last changes fastest.
Arguments:
- momentum: float32 [8192, 28672], P('fsdp', 'tensor'), may hold values from -405 to 405
- gradient: bfloat16 [8192, 28672], P('fsdp', 'tensor'), may hold values from -6 to 6
- basis: float32 [28672, 256], P('tensor', 'fsdp'), may hold values from -0.03125 to 0.03125
Outputs:
- new_momentum: float32 [8192, 28672], P('fsdp', 'tensor')
- orthonormal: float32 [8192, 256], P('fsdp')
- new_basis: float32 [28672, 256], P('tensor', 'fsdp')
All inputs are finite; a program needn't handle non-finite values.
Results may differ from a plain program's by a relative error of at most 0.0003.
Values sent between devices are 32-bit elements; how exact they have to be, the bound alone decides.
No kernel may reach another device: no remote copies, remote signals or barrier semaphores. Data moves between devices by JAX's collectives and lax.ppermute only.
A program may use at most 64 MiB of HBM per device.

v0:
```python
import jax
import jax.numpy as jnp
from jax import lax
from jax.sharding import PartitionSpec as P

momentum_keep = 0.95
column_eps = 1e-08


def on_device(momentum, gradient, basis):
    high = lax.Precision.HIGHEST
    buffer = momentum + gradient.astype(jnp.float32)
    partial_left = jnp.dot(
        buffer,
        lax.all_gather(basis, "fsdp", axis=1, tiled=True),
        precision=high,
        preferred_element_type=jnp.float32,
    )
    left_raw = lax.psum(partial_left, "tensor")
    gram_matrix = lax.psum(
        lax.dot_general(
            left_raw,
            left_raw,
            (((0,), (0,)), ((), ())),
            precision=high,
            preferred_element_type=jnp.float32,
        ),
        "fsdp",
    )
    factor = jnp.linalg.cholesky(gram_matrix)
    orthonormal = jax.scipy.linalg.solve_triangular(factor, left_raw.T, lower=True).T
    term = lax.dot_general(
        buffer,
        orthonormal,
        (((0,), (0,)), ((), ())),
        precision=high,
        preferred_element_type=jnp.float32,
    )
    right_raw = lax.psum(term, "fsdp")
    squares = lax.psum(jnp.sum(right_raw * right_raw, axis=0), "tensor")
    scaled = right_raw / (jnp.sqrt(squares) + column_eps)
    columns = basis.shape[1]
    new_basis = lax.dynamic_slice_in_dim(scaled, lax.axis_index("fsdp") * columns, columns, 1)
    feedback = lax.dot_general(
        orthonormal,
        right_raw,
        (((1,), (1,)), ((), ())),
        precision=high,
        preferred_element_type=jnp.float32,
    )
    new_momentum = buffer - (1.0 - momentum_keep) * feedback
    return (new_momentum, orthonormal, new_basis)


def solution(mesh):
    placed = (P("fsdp", "tensor"), P("fsdp", "tensor"), P("tensor", "fsdp"))
    return jax.shard_map(
        on_device,
        mesh=mesh,
        in_specs=placed,
        out_specs=(P("fsdp", "tensor"), P("fsdp", None), P("tensor", "fsdp")),
        check_vma=False,
    )
```

profile of v0, /device:TPU:1, one launch (start us, length us, event | category | flops | bytes accessed | tf_op | source)
XLA Modules:
  0.0 897.6 jit_solution(4143879030097302909)
XLA Ops:
  7.2 0.0 all-gather.3.cloned.1.call-start
  7.2 0.7 all-gather.3.cloned.1.call-update
  7.9 0.0 copy-start
  7.9 0.0 copy-start.1
  7.9 0.0 all-reduce.5.cloned.1.call-start
  8.0 144.3 %all-gather.3.cloned.1.call-done = f32[64,4,3584]{2,1,0:T(4,128)} async-done(((f32[1,4,3584]{2,1,0:T(4,128)}), f32[64,4,3584]{2,1,0:T(4,128)}) %all-gather.3.cloned.1.call-update) | async-done | bytes 3670032 | tf_op jit(solution)/shard_map/all_gather | solution.py:15
  152.3 5.3 reshape.46
  157.6 0.0 copy-done
  157.6 0.0 copy-done.1
  157.6 6.4 fusion.2
  164.0 0.0 all-reduce.5.cloned.1.call-update
  164.0 0.0 all-reduce.7.cloned.1.call-start
  164.1 77.0 %all-reduce.5.cloned.1.call-done = f32[128,256]{1,0:T(8,128)} async-done(((f32[128,256]{1,0:T(8,128)}), f32[128,256]{1,0:T(8,128)}) %all-reduce.5.cloned.1.call-update) | async-done | bytes 131088 | tf_op jit(solution)/shard_map/psum | solution.py:19
  241.1 2.1 fusion.15
  243.2 0.0 all-reduce.7.cloned.1.call-update
  243.2 0.2 all-reduce.9.cloned.1.call-start
  243.5 255.3 %all-reduce.7.cloned.1.call-done = f32[256,256]{0,1:T(8,128)} async-done(((f32[256,256]{0,1:T(8,128)}), f32[256,256]{0,1:T(8,128)}) %all-reduce.7.cloned.1.call-update) | async-done | bytes 262160 | tf_op jit(solution)/shard_map/psum | solution.py:20
  498.8 1.1 copy.11
  499.9 0.0 copy-start.2
  499.9 1.0 fusion.3
  501.0 0.0 copy-start.3
  501.0 0.7 copy-done.3
  501.7 11.7 %cholesky.50 = f32[128,128]{1,0:T(8,128)S(1)} custom-call(f32[128,128]{1,0:T(8,128)S(1)} %cholesky.118), custom_call_target="Cholesky" | custom-call | tf_op jit(solution)/shard_map/jit(cholesky)/cholesky | solution.py:30
  513.4 9.8 %custom-call.15 = f32[1,128,128]{1,2,0:T(8,128)S(1)} custom-call(f32[1,128,128]{2,1,0:T(8,128)S(1)} %get-tuple-element.30), custom_call_target="InvertDiagBlocksLowerTriangular" | custom-call | tf_op jit(solution)/shard_map/jit(cholesky)/cholesky | solution.py:30
  523.3 1.0 constant_dynamic-update-slice_fusion
  524.3 1.1 convolution_subtract_fusion.1
  525.4 11.7 %cholesky.105 = f32[128,128]{1,0:T(8,128)S(1)} custom-call(f32[128,128]{1,0:T(8,128)S(1)} %convolution_subtract_fusion.1), custom_call_target="Cholesky" | custom-call | tf_op jit(solution)/shard_map/jit(cholesky)/cholesky | solution.py:30
  537.2 0.7 compare_reduce_fusion
  539.3 0.1 triangular_solve.57
  539.4 5.5 while.1
  539.5 0.6 fusion.25
  540.1 2.1 bitcast_dynamic-update-slice_fusion.2
  542.2 0.6 fusion.25
  542.8 2.1 bitcast_dynamic-update-slice_fusion.2
  544.9 20.5 %custom-call.16 = f32[2,128,128]{1,2,0:T(8,128)S(1)} custom-call(f32[2,128,128]{2,1,0:T(8,128)} %get-tuple-element.10), custom_call_target="InvertDiagBlocksLowerTriangular" | custom-call | tf_op jit(solution)/shard_map/jit(_solve_triangular)/triangular_solve | solution.py:31
  565.3 0.0 copy-done.2
  565.4 0.3 fusion.7
  565.6 0.3 convolution_subtract_fusion
  565.9 0.3 fusion.6
  566.2 4.9 fusion.1
  571.2 0.0 all-reduce.9.cloned.1.call-update
  571.2 0.8 copy.12
  572.0 281.5 %all-reduce.9.cloned.1.call-done = f32[3584,256]{1,0:T(8,128)} async-done(((f32[3584,256]{1,0:T(8,128)}), f32[3584,256]{1,0:T(8,128)}) %all-reduce.9.cloned.1.call-update) | async-done | bytes 3670032 | tf_op jit(solution)/shard_map/psum | solution.py:39
  853.5 2.5 multiply_reduce_fusion
  856.0 21.8 %psum.31 = f32[256]{0:T(256)S(1)} all-reduce(f32[256]{0:T(256)S(1)} %multiply_reduce_fusion), channel_id=1, replica_groups=mesh['fsdp'=64,'tensor'=8] {'tensor'}, use_global_device_ids=true, to_apply=%region_8.9 | all-reduce | flops 256 | bytes 2048 | tf_op jit(solution)/shard_map/psum | solution.py:40
  877.8 0.1 dynamic-slice.3
  877.9 3.3 dynamic-slice_divide_fusion
  881.2 2.7 copy.13
  883.8 7.2 fusion
  (11 shorter events, 0.2 us)
Async XLA Ops:
  7.2 145.2 %all-gather.3.cloned.1.call-start = ((), (), s32[]{:S(2)}) async-start(), calls=%async_computation.3 | async-start | bytes 3727360 | tf_op jit(solution)/shard_map/all_gather | solution.py:15
  7.9 149.7 %copy-start = (f32[128,3584]{1,0:T(8,128)S(1)}, f32[128,3584]{1,0:T(8,128)}, u32[]{:S(2)}) copy-start(f32[128,3584]{1,0:T(8,128)} %param.3) | copy-start | bytes 5505028
  7.9 149.7 %copy-start.1 = (bf16[128,3584]{1,0:T(8,128)(2,1)S(1)}, bf16[128,3584]{1,0:T(8,128)(2,1)}, u32[]{:S(2)}) copy-start(bf16[128,3584]{1,0:T(8,128)(2,1)} %param.4) | copy-start | bytes 2752516
  7.9 233.2 %all-reduce.5.cloned.1.call-start = ((), (), s32[]{:S(2)}) async-start(), calls=%async_computation | async-start | bytes 262144 | tf_op jit(solution)/shard_map/psum | solution.py:19
  164.0 334.8 %all-reduce.7.cloned.1.call-start = ((), (), s32[]{:S(2)}) async-start(), calls=%async_computation.1 | async-start | bytes 524288 | tf_op jit(solution)/shard_map/psum | solution.py:20
  243.2 610.2 %all-reduce.9.cloned.1.call-start = ((), (), s32[]{:S(2)}) async-start(), calls=%async_computation.2 | async-start | bytes 7340032 | tf_op jit(solution)/shard_map/psum | solution.py:39
  499.9 65.4 %copy-start.2 = (f32[128,256]{1,0:T(8,128)S(1)}, f32[128,256]{1,0:T(8,128)}, u32[]{:S(2)}) copy-start(f32[128,256]{1,0:T(8,128)} %all-reduce.5.cloned.1.call-done) | copy-start | bytes 393220
  501.0 0.7 copy-start.3
Sparse Core Ops, SparseCore 0:
  10.9 141.3 all-gather.2
  164.2 76.9 all-reduce.4
  245.5 253.2 all-reduce.6
  571.3 282.1 all-reduce.8
where the time goes:
time: 898 us
  waiting for transfers between devices  759 us (85%)
  other arithmetic  61.4 us (7%)
  matrix products  23.6 us (3%)
  blocking collectives  21.8 us (2%)
  local copies, waits for them, and re-layouts  16 us (2%)
  between operations  15.3 us (2%)
    psum x1, waiting for transfers between devices, on_device(): right_raw = lax.psum(term, 'fsdp')  282 us
    psum x1, waiting for transfers between devices, on_device(): lax.psum(lax.dot_general(left_raw, left_raw, (((0,), (0,)), ((), ())), pr...  255 us
    all_gather x1, waiting for transfers between devices, on_device(): lax.all_gather(basis, 'fsdp', axis=1, tiled=True)  144 us
    psum x1, waiting for transfers between devices, on_device(): left_raw = lax.psum(partial_left, 'tensor')  77 us
    another operation x6, other arithmetic, on_device(): factor = jnp.linalg.cholesky(gram_matrix)  34 us
    psum x1, blocking collectives, on_device(): squares = lax.psum(jnp.sum(right_raw * right_raw, axis=0), 'tensor')  21.8 us
    another operation x3, other arithmetic, on_device(): jax.scipy.linalg.solve_triangular(factor, left_raw.T, lower=True)  20.5 us
  transfers between devices with their start and end apart: 4, of which 4 were waited for; matrix products, arithmetic and copies ran while one was open for 0% of the time, Pallas kernels for 0%

commit v1 on v0

v1 whole, which is shorter than its diff:
```python
import jax
import jax.numpy as jnp
from jax import lax
from jax.experimental import pallas as pl
from jax.experimental.pallas import tpu as pltpu
from jax.sharding import Mesh
from jax.sharding import PartitionSpec as P

momentum_keep = 0.95
column_eps = 1e-08
high = lax.Precision.HIGHEST

Z = ("zh", "zl")
GROUP = ("x", "y", "core")
HALF = 128


def dot(a, b, contract, precision=high):
    return lax.dot_general(
        a, b, ((contract[:1], contract[1:]), ((), ())), precision=precision, preferred_element_type=jnp.float32
    )


def inverse_factor_block(block):
    n = block.shape[0]
    groups = [block[8 * g : 8 * g + 8, :] for g in range(n // 8)]
    lane = lax.broadcasted_iota(jnp.int32, (1, n), 1)
    row_in_group = lax.broadcasted_iota(jnp.int32, (8, n), 0)
    for k in range(0, n, 4):
        first, at = k // 8, k % 8
        inside = (lane >= k) & (lane < k + 4)
        cols = {
            g: [jnp.broadcast_to(groups[g][:, k + j : k + j + 1], (8, n)) for j in range(4)]
            for g in range(first, n // 8)
        }
        a = [[cols[first][j][at + i : at + i + 1, :] for j in range(i + 1)] for i in range(4)]
        low = [[None] * 4 for _ in range(4)]
        inv = [[None] * 4 for _ in range(4)]
        for j in range(4):
            pivot = a[j][j]
            for m in range(j):
                pivot = pivot - low[j][m] * low[j][m]
            r = lax.rsqrt(pivot)
            r = r * (1.5 - 0.5 * (pivot * r) * r)
            inv[j][j] = r
            for i in range(j + 1, 4):
                value = a[i][j]
                for m in range(j):
                    value = value - low[i][m] * low[j][m]
                low[i][j] = value * r
        for j in range(4):
            for i in range(j + 1, 4):
                value = low[i][j] * inv[j][j]
                for m in range(j + 1, i):
                    value = value + low[i][m] * inv[m][j]
                inv[i][j] = -(value * inv[i][i])
        rows = []
        for i in range(4):
            unit = jnp.where(lane == k + i, 1.0, 0.0)
            rows.append(jnp.where(inside, unit, groups[first][at + i : at + i + 1, :]))
        new = []
        for j in range(4):
            value = inv[j][0] * rows[0]
            for i in range(1, j + 1):
                value = value + inv[j][i] * rows[i]
            new.append(value)
        for g in range(first, n // 8):
            if g == first and at == 4:
                updated = groups[g]
            else:
                updated = jnp.where(inside, 0.0, groups[g])
                for j in range(4):
                    factor = inv[j][0] * cols[g][0]
                    for i in range(1, j + 1):
                        factor = factor + inv[j][i] * cols[g][i]
                    updated = updated - factor * new[j]
            if g == first:
                if at == 4:
                    updated = groups[g]
                for j in range(4):
                    updated = jnp.where(row_in_group == at + j, new[j], updated)
            groups[g] = updated
    whole = jnp.concatenate(groups, axis=0)
    rows_at = lax.broadcasted_iota(jnp.int32, (n, n), 0)
    cols_at = lax.broadcasted_iota(jnp.int32, (n, n), 1)
    return jnp.where(rows_at >= cols_at, whole, 0.0)


def inverse_factor_kernel(gram_ref, out_ref):
    top = slice(0, HALF)
    low = slice(HALF, 2 * HALF)
    x11 = inverse_factor_block(gram_ref[top, top])
    u = dot(x11, gram_ref[top, low], (1, 0))
    rest = gram_ref[low, low] - dot(u, u, (0, 0))
    t = dot(u, x11, (0, 0))
    x22 = inverse_factor_block(rest)
    out_ref[top, top] = x11
    out_ref[top, low] = jnp.zeros((HALF, HALF), jnp.float32)
    out_ref[low, top] = -dot(x22, t, (1, 0))
    out_ref[low, low] = x22


def inverse_factor(gram):
    vmem = pl.BlockSpec(memory_space=pltpu.VMEM)
    return pl.pallas_call(
        inverse_factor_kernel,
        out_shape=jax.ShapeDtypeStruct(gram.shape, jnp.float32),
        in_specs=[vmem],
        out_specs=vmem,
        compiler_params=pltpu.CompilerParams(vmem_limit_bytes=16 << 20),
        cost_estimate=pl.CostEstimate(flops=2 * 256**3, bytes_accessed=2 * 256 * 256 * 4, transcendentals=256),
    )(gram)


def on_device(momentum, gradient, basis):
    rows, columns = momentum.shape
    ranks = basis.shape[1]
    rank = 256
    nx, ny = lax.axis_size("x"), lax.axis_size("y")
    nzh, nzl = lax.axis_size("zh"), lax.axis_size("zl")
    nz = nzh * nzl
    part = columns // nx
    x_at, y_at = lax.axis_index("x"), lax.axis_index("y")

    buffer = momentum + gradient.astype(jnp.float32)
    tall = lax.all_to_all(buffer.reshape(rows, nx, part).transpose(1, 0, 2), "x", 0, 0, tiled=True)
    tall = tall.reshape(nx * rows, part)
    v = lax.all_to_all(basis.T.reshape(ranks, nx, part).transpose(1, 0, 2), "x", 0, 0, tiled=True)
    v = lax.all_gather(v.reshape(nx * ranks, part), Z, axis=0, tiled=True)

    partial = dot(tall, v, (1, 1))
    peers = lax.axis_size(GROUP)
    piece = partial.shape[0] // peers
    parts = lax.all_to_all(partial.reshape(peers, piece, rank), GROUP, 0, 0, tiled=True)
    own = jnp.sum(parts, axis=0)
    left = lax.all_to_all(jnp.broadcast_to(own[None], (peers, piece, rank)), GROUP, 0, 0, tiled=True)
    left = left.reshape(nx * rows, rank)

    slab = rank // ny
    w_part = dot(left, tall, (0, 0))
    g_part = dot(left, lax.dynamic_slice_in_dim(left, y_at * slab, slab, 1), (0, 0))
    both = jnp.concatenate([w_part, g_part], axis=1).reshape(nzh, nzl, rank // nz, part + slab)
    both = jnp.sum(lax.all_to_all(both, "zl", 1, 1, tiled=True), axis=1)
    both = jnp.sum(lax.all_to_all(both, "zh", 0, 0, tiled=True), axis=0)
    both = lax.all_gather(both, Z, axis=0, tiled=True)
    w = both[:, :part]
    gram = lax.all_gather(both[:, part:].T, "y", axis=0, tiled=True)
    inverse = inverse_factor((gram + gram.T) * 0.5)

    ortho = dot(left, inverse, (1, 1))
    orthonormal = lax.dynamic_slice_in_dim(ortho, x_at * rows, rows, 0)
    right = dot(inverse, w, (1, 0))

    z_at = lax.axis_index(Z)
    mine = lax.dynamic_slice_in_dim(right, z_at * (nx * ranks), nx * ranks, 0)
    mine = lax.all_to_all(mine.reshape(nx, ranks, part), "x", 0, 0, tiled=True)
    mine = mine.transpose(1, 0, 2).reshape(ranks, columns)
    squares = lax.psum(jnp.sum(mine * mine, axis=1), ("y", "core"))
    new_basis = (mine / (jnp.sqrt(squares) + column_eps)[:, None]).T

    feedback = dot(ortho, right, (1, 0))
    feedback = lax.all_to_all(feedback.reshape(nx, rows, part), "x", 0, 0, tiled=True)
    feedback = feedback.transpose(1, 0, 2).reshape(rows, columns)
    new_momentum = buffer - (1.0 - momentum_keep) * feedback
    return (new_momentum, orthonormal, new_basis)


def solution(mesh):
    fine = Mesh(mesh.devices.reshape(4, 4, 4, 4, 2), ("zh", "zl", "x", "y", "core"))
    fsdp, tensor = ("zh", "zl", "x"), ("y", "core")
    return jax.shard_map(
        on_device,
        mesh=fine,
        in_specs=(P(fsdp, tensor), P(fsdp, tensor), P(tensor, fsdp)),
        out_specs=(P(fsdp, tensor), P(fsdp, None), P(tensor, fsdp)),
        check_vma=False,
    )
```

time: 898 us -> 246 us (0.27)
  waiting for transfers between devices: 759 us -> 28.6 us
  blocking collectives: 21.8 us -> 155 us
  other arithmetic: 61.4 us -> 5.32 us
  starting transfers between devices: 0.34 us -> 25.5 us
  between operations: 15.3 us -> 0.82 us
  Pallas kernels: 0 us -> 14.2 us
  matrix products: 23.6 us -> 9.52 us
  local copies, waits for them, and re-layouts: 16 us -> 6.61 us
    psum x3 -> x0, waiting for transfers between devices: 614 us -> none  [the longest x1 282 us: on_device(): right_raw = lax.psum(term, 'fsdp')]
    all_gather x1 -> x0, waiting for transfers between devices: 144 us -> none  [on_device(): lax.all_gather(basis, 'fsdp', axis=1, tiled=True)]
    all_gather x0 -> x3, blocking collectives: none -> 74 us  [the longest x1 34.9 us: on_device(): v = lax.all_gather(v.reshape(nx * ranks, part), Z, axis=0, tiled=True)]
    all_to_all x0 -> x2, blocking collectives: none -> 55.4 us  [the longest x1 28.4 us: on_device(): both = jnp.sum(lax.all_to_all(both, 'zl', 1, 1, tiled=True), axis=1)]
    another operation x9 -> x0, other arithmetic: 54.5 us -> none  [the longest x6 34 us: on_device(): factor = jnp.linalg.cholesky(gram_matrix)]
    all_to_all x0 -> x6, waiting for transfers between devices: none -> 28.6 us  [the longest x1 15.7 us: on_device(): both = jnp.sum(lax.all_to_all(both, 'zh', 0, 0, tiled=True), axis=0)]
    all_to_all x0 -> x6, starting transfers between devices: none -> 25.5 us  [the longest x1 5.89 us: on_device(): both = jnp.sum(lax.all_to_all(both, 'zh', 0, 0, tiled=True), axis=0)]
    pallas_call x0 -> x1, Pallas kernels: none -> 14.2 us  [inverse_factor(): pl.pallas_call(inverse_factor_kernel, out_shape=jax.ShapeDtypeStruct(gram...]
  transfers between devices with their start and end apart: 4 -> 6, of which waited for: 4 -> 3; matrix products, arithmetic and copies ran while one was open for 0% -> 3% of each run, Pallas kernels for 0% -> 0%
where the time goes in v1:
time: 246 us; the launch traced here: 245 us
  blocking collectives  155 us (63%)
  waiting for transfers between devices  28.6 us (12%)
  starting transfers between devices  25.5 us (10%)
  Pallas kernels  14.2 us (6%)
  matrix products  9.52 us (4%)
  local copies, waits for them, and re-layouts  6.61 us (3%)
  other arithmetic  5.32 us (2%)
    all_gather x1, blocking collectives, on_device(): v = lax.all_gather(v.reshape(nx * ranks, part), Z, axis=0, tiled=True)  34.9 us
    all_gather x1, blocking collectives, on_device(): both = lax.all_gather(both, Z, axis=0, tiled=True)  29.3 us
    all_to_all x1, blocking collectives, on_device(): both = jnp.sum(lax.all_to_all(both, 'zl', 1, 1, tiled=True), axis=1)  28.4 us
    all_to_all x1, blocking collectives, on_device(): lax.all_to_all(partial.reshape(peers, piece, rank), GROUP, 0, 0, tiled=True)  26.9 us
    psum x1, blocking collectives, on_device(): squares = lax.psum(jnp.sum(mine * mine, axis=1), ('y', 'core'))  25.5 us
    all_to_all x1, waiting for transfers between devices, on_device(): both = jnp.sum(lax.all_to_all(both, 'zh', 0, 0, tiled=True), axis=0)  15.7 us
    pallas_call x1, Pallas kernels, inverse_factor(): pl.pallas_call(inverse_factor_kernel, out_shape=jax.ShapeDtypeStruct(gram...  14.2 us
    all_to_all x1, waiting for transfers between devices, on_device(): lax.all_to_all(jnp.broadcast_to(own[None], (peers, piece, rank)), GROUP,...  11.6 us
  transfers between devices with their start and end apart: 6, of which 3 were waited for; matrix products, arithmetic and copies ran while one was open for 3% of the time, Pallas kernels for 0%

profile of v1, /device:TPU:1, one launch (start us, length us, event | category | flops | bytes accessed | tf_op | source)
XLA Modules:
  0.0 245.5 jit_solution(1213328028695197261)
XLA Ops:
  0.6 4.9 %all-to-all-start.1 = ((f32[4,4,896]{2,1,0:T(4,128)}), f32[4,4,896]{2,1,0:T(4,128)S(1)}, u32[]{:S(2)}, u32[]{:S(2)}) async-start(f32[4,4,896]{2,1,0:T(4,128)} %bitcast.57), calls=%async_computation.1 | async-start | bytes 114688 | tf_op jit(solution)/shard_map/all_to_all | solution.py:128
  5.5 1.9 convert_add_fusion
  7.4 0.0 copy-start
  7.4 1.2 copy-done
  8.6 1.4 copy.40
  10.0 0.0 all-to-all-done.1
  10.0 4.2 %all-to-all-start = ((f32[4,128,896]{2,1,0:T(8,128)}), f32[4,128,896]{2,1,0:T(8,128)S(1)}, u32[]{:S(2)}, u32[]{:S(2)}) async-start(f32[4,128,896]{2,1,0:T(8,128)} %bitcast.53), calls=%async_computation | async-start | bytes 3670016 | tf_op jit(solution)/shard_map/all_to_all | solution.py:126
  14.3 34.9 %all_gather.9 = f32[256,896]{1,0:T(8,128)S(1)} all-gather(f32[16,896]{1,0:T(8,128)S(1)} %reshape.43), channel_id=1, replica_groups=mesh['zh'=4,'zl'=4,'x'=4,'y'=4,'core'=2] {'zh','zl'}, dimensions={0}, use_global_device_ids=true | all-gather | bytes 974848 | tf_op jit(solution)/shard_map/all_gather | solution.py:129
  49.1 0.0 all-to-all-done
  49.1 1.8 fusion.2
  50.9 26.9 %all_to_all.40 = f32[32,16,256]{2,1,0:T(8,128)S(1)} all-to-all(f32[32,16,256]{2,1,0:T(8,128)S(1)} %fusion.2), channel_id=1, replica_groups=mesh['zh'=4,'zl'=4,'x'=4,'y'=4,'core'=2] {'x','y','core'}, dimensions={0} | all-to-all | bytes 1048576 | tf_op jit(solution)/shard_map/all_to_all | solution.py:134
  77.9 0.9 broadcast_in_dim.2
  78.8 3.7 %all-to-all-start.3 = ((f32[32,16,256]{2,1,0:T(8,128)}), f32[32,16,256]{2,1,0:T(8,128)S(1)}, u32[]{:S(2)}, u32[]{:S(2)}) async-start(f32[32,16,256]{2,1,0:T(8,128)} %broadcast_in_dim.2), calls=%async_computation.3 | async-start | bytes 1048576 | tf_op jit(solution)/shard_map/all_to_all | solution.py:136
  82.5 11.6 %all-to-all-done.3 = f32[32,16,256]{2,1,0:T(8,128)S(1)} async-done(((f32[32,16,256]{2,1,0:T(8,128)}), f32[32,16,256]{2,1,0:T(8,128)S(1)}, u32[]{:S(2)}, u32[]{:S(2)}) %all-to-all-start.3) | async-done | bytes 524320 | tf_op jit(solution)/shard_map/all_to_all | solution.py:136
  94.0 1.1 fusion.5
  95.1 1.9 fusion.9
  97.0 0.1 pad_maximum_fusion
  97.1 0.1 copy.32
  97.3 28.4 %all_to_all.41 = f32[4,4,16,960]{3,2,0,1:T(8,128)S(1)} all-to-all(f32[4,4,16,960]{3,2,0,1:T(8,128)S(1)} %copy.32), channel_id=1, replica_groups=mesh['zh'=4,'zl'=4,'x'=4,'y'=4,'core'=2] {'zl'}, dimensions={1} | all-to-all | bytes 1966080 | tf_op jit(solution)/shard_map/all_to_all | solution.py:143
  125.7 0.8 reduce_sum.37
  126.5 5.9 %all-to-all-start.5 = ((f32[4,16,960]{2,1,0:T(8,128)}), f32[4,16,960]{2,1,0:T(8,128)S(1)}, u32[]{:S(2)}, u32[]{:S(2)}) async-start(f32[4,16,960]{2,1,0:T(8,128)} %reduce_sum.37), calls=%async_computation.5 | async-start | bytes 524288 | tf_op jit(solution)/shard_map/all_to_all | solution.py:144
  132.4 15.7 %all-to-all-done.5 = f32[4,16,960]{2,1,0:T(8,128)S(1)} async-done(((f32[4,16,960]{2,1,0:T(8,128)}), f32[4,16,960]{2,1,0:T(8,128)S(1)}, u32[]{:S(2)}, u32[]{:S(2)}) %all-to-all-start.5) | async-done | bytes 245792 | tf_op jit(solution)/shard_map/all_to_all | solution.py:144
  148.1 29.3 %all_gather.10 = f32[256,960]{1,0:T(8,128)S(1)} all-gather(f32[16,960]{1,0:T(8,128)S(1)} %reduce_sum.38), channel_id=1, replica_groups=mesh['zh'=4,'zl'=4,'x'=4,'y'=4,'core'=2] {'zh','zl'}, dimensions={0}, use_global_device_ids=true | all-gather | bytes 1044480 | tf_op jit(solution)/shard_map/all_gather | solution.py:145
  177.4 0.1 copy.33
  177.5 9.8 %all_gather.11 = f32[256,256]{1,0:T(8,128)S(1)} all-gather(f32[64,256]{1,0:T(8,128)S(1)} %copy.33), channel_id=1, replica_groups=mesh['zh'=4,'zl'=4,'x'=4,'y'=4,'core'=2] {'y'}, dimensions={0}, use_global_device_ids=true | all-gather | bytes 327680 | tf_op jit(solution)/shard_map/all_gather | solution.py:147
  187.4 0.1 copy.34
  187.5 14.2 %shard_map.58 = f32[256,256]{1,0:T(8,128)S(1)} custom-call(f32[256,256]{1,0:T(8,128)S(1)} %fusion.4.gram_ref), custom_call_target="tpu_custom_call" | custom-call | flops 33554432 | bytes 524288 | tf_op jit(solution)/shard_map/pallas_call | solution.py:105
  201.7 1.0 fusion
  202.7 0.6 fusion.10
  203.4 0.6 reshape.48
  204.0 3.3 %all-to-all-start.7 = ((f32[4,4,896]{2,1,0:T(4,128)}), f32[4,4,896]{2,1,0:T(4,128)S(1)}, u32[]{:S(2)}, u32[]{:S(2)}) async-start(f32[4,4,896]{2,1,0:T(4,128)} %reshape.48), calls=%async_computation.7 | async-start | bytes 114688 | tf_op jit(solution)/shard_map/all_to_all | solution.py:156
  207.3 3.1 %fusion.11 = f32[512,896]{1,0:T(8,128)} fusion(f32[512,256]{1,0:T(8,128)S(1)} %fusion.10, f32[256,896]{1,0:T(8,128)S(1)} %fusion), kind=kOutput, calls=%fused_computation.22 | convolution fusion | flops 1409286144 | bytes 3276800 | tf_op jit(solution)/shard_map/dot_general | solution.py:19
  210.4 1.3 all-to-all-done.7
  211.7 3.6 %all-to-all-start.6 = ((f32[4,128,896]{2,1,0:T(8,128)}), f32[4,128,896]{2,1,0:T(8,128)S(1)}, u32[]{:S(2)}, u32[]{:S(2)}) async-start(f32[4,128,896]{2,1,0:T(8,128)} %bitcast.11), calls=%async_computation.6 | async-start | bytes 3670016 | tf_op jit(solution)/shard_map/all_to_all | solution.py:162
  215.3 0.1 fusion.7
  215.5 0.7 constant_dynamic-slice_fusion.1
  216.1 25.5 %psum.7 = f32[4]{0:T(128)S(1)} all-reduce(f32[4]{0:T(128)S(1)} %fusion.7), channel_id=1, replica_groups=mesh['zh'=4,'zl'=4,'x'=4,'y'=4,'core'=2] {'y','core'}, use_global_device_ids=true, to_apply=%region_4.0 | all-reduce | flops 4 | bytes 32 | tf_op jit(solution)/shard_map/psum | solution.py:158
  241.7 0.7 divide_bitcast_fusion
  242.4 0.0 all-to-all-done.6
  242.4 0.2 multiply_bitcast_fusion
  242.6 0.0 copy-start.1
  242.6 0.2 copy.38
  242.8 1.3 copy-done.1
  244.1 1.4 sub.3
  (7 shorter events, 0.2 us)
Async XLA Ops:
  0.6 9.4 %all-to-all-start.1 = ((f32[4,4,896]{2,1,0:T(4,128)}), f32[4,4,896]{2,1,0:T(4,128)S(1)}, u32[]{:S(2)}, u32[]{:S(2)}) async-start(f32[4,4,896]{2,1,0:T(4,128)} %bitcast.57), calls=%async_computation.1 | async-start | bytes 114688 | tf_op jit(solution)/shard_map/all_to_all | solution.py:128
  7.4 1.2 copy-start
  10.0 39.1 %all-to-all-start = ((f32[4,128,896]{2,1,0:T(8,128)}), f32[4,128,896]{2,1,0:T(8,128)S(1)}, u32[]{:S(2)}, u32[]{:S(2)}) async-start(f32[4,128,896]{2,1,0:T(8,128)} %bitcast.53), calls=%async_computation | async-start | bytes 3670016 | tf_op jit(solution)/shard_map/all_to_all | solution.py:126
  78.8 15.3 %all-to-all-start.3 = ((f32[32,16,256]{2,1,0:T(8,128)}), f32[32,16,256]{2,1,0:T(8,128)S(1)}, u32[]{:S(2)}, u32[]{:S(2)}) async-start(f32[32,16,256]{2,1,0:T(8,128)} %broadcast_in_dim.2), calls=%async_computation.3 | async-start | bytes 1048576 | tf_op jit(solution)/shard_map/all_to_all | solution.py:136
  126.5 21.6 %all-to-all-start.5 = ((f32[4,16,960]{2,1,0:T(8,128)}), f32[4,16,960]{2,1,0:T(8,128)S(1)}, u32[]{:S(2)}, u32[]{:S(2)}) async-start(f32[4,16,960]{2,1,0:T(8,128)} %reduce_sum.37), calls=%async_computation.5 | async-start | bytes 524288 | tf_op jit(solution)/shard_map/all_to_all | solution.py:144
  204.0 7.7 %all-to-all-start.7 = ((f32[4,4,896]{2,1,0:T(4,128)}), f32[4,4,896]{2,1,0:T(4,128)S(1)}, u32[]{:S(2)}, u32[]{:S(2)}) async-start(f32[4,4,896]{2,1,0:T(4,128)} %reshape.48), calls=%async_computation.7 | async-start | bytes 114688 | tf_op jit(solution)/shard_map/all_to_all | solution.py:156
  211.7 30.7 %all-to-all-start.6 = ((f32[4,128,896]{2,1,0:T(8,128)}), f32[4,128,896]{2,1,0:T(8,128)S(1)}, u32[]{:S(2)}, u32[]{:S(2)}) async-start(f32[4,128,896]{2,1,0:T(8,128)} %bitcast.11), calls=%async_computation.6 | async-start | bytes 3670016 | tf_op jit(solution)/shard_map/all_to_all | solution.py:162
  242.6 1.5 copy-start.1

commit v2 on v1

--- a/solution.py
+++ b/solution.py
@@ -1,3 +1,5 @@
+import functools
+
 import jax
 import jax.numpy as jnp
 from jax import lax
@@ -13,6 +15,7 @@
 Z = ("zh", "zl")
 GROUP = ("x", "y", "core")
 HALF = 128
+LANES = 128
 
 
 def dot(a, b, contract, precision=high):
@@ -41,7 +44,6 @@
             for m in range(j):
                 pivot = pivot - low[j][m] * low[j][m]
             r = lax.rsqrt(pivot)
-            r = r * (1.5 - 0.5 * (pivot * r) * r)
             inv[j][j] = r
             for i in range(j + 1, 4):
                 value = a[i][j]
@@ -86,82 +88,202 @@
     return jnp.where(rows_at >= cols_at, whole, 0.0)
 
 
-def inverse_factor_kernel(gram_ref, out_ref):
-    top = slice(0, HALF)
-    low = slice(HALF, 2 * HALF)
-    x11 = inverse_factor_block(gram_ref[top, top])
-    u = dot(x11, gram_ref[top, low], (1, 0))
-    rest = gram_ref[low, low] - dot(u, u, (0, 0))
+def inverse_factor(gram):
+    x11 = inverse_factor_block(gram[:HALF, :HALF])
+    u = dot(x11, gram[:HALF, HALF:], (1, 0))
+    rest = gram[HALF:, HALF:] - dot(u, u, (0, 0))
     t = dot(u, x11, (0, 0))
     x22 = inverse_factor_block(rest)
-    out_ref[top, top] = x11
-    out_ref[top, low] = jnp.zeros((HALF, HALF), jnp.float32)
-    out_ref[low, top] = -dot(x22, t, (1, 0))
-    out_ref[low, low] = x22
-
-
-def inverse_factor(gram):
+    return x11, -dot(x22, t, (1, 0)), x22
+
+
+def split_kernel(momentum_ref, gradient_ref, out_ref):
+    out_ref[0] = momentum_ref[...] + gradient_ref[...].astype(jnp.float32)
+
+
+def split(momentum, gradient, parts):
+    rows, columns = momentum.shape
+    part = columns // parts
+    block = pl.BlockSpec((rows, part), lambda i: (0, i))
+    return pl.pallas_call(
+        split_kernel,
+        grid=(parts,),
+        out_shape=jax.ShapeDtypeStruct((parts, rows, part), jnp.float32),
+        in_specs=[block, block],
+        out_specs=pl.BlockSpec((1, rows, part), lambda i: (i, 0, 0)),
+        compiler_params=pltpu.CompilerParams(vmem_limit_bytes=16 << 20),
+        cost_estimate=pl.CostEstimate(flops=momentum.size, bytes_accessed=10 * momentum.size, transcendentals=0),
+    )(momentum, gradient)
+
+
+def join_kernel(buffer_ref, back_ref, squares_ref, momentum_ref, basis_ref):
+    rows = momentum_ref.shape[0]
+    momentum_ref[...] = buffer_ref[0] - (1.0 - momentum_keep) * back_ref[0, :rows, :]
+    basis_ref[...] = back_ref[0, rows:, :] / (jnp.sqrt(squares_ref[...]) + column_eps)
+
+
+def join(buffer, back, squares):
+    parts, rows, part = buffer.shape
+    ranks = back.shape[1] - rows
+    return pl.pallas_call(
+        join_kernel,
+        grid=(parts,),
+        out_shape=(
+            jax.ShapeDtypeStruct((rows, parts * part), jnp.float32),
+            jax.ShapeDtypeStruct((ranks, parts * part), jnp.float32),
+        ),
+        in_specs=[
+            pl.BlockSpec((1, rows, part), lambda i: (i, 0, 0)),
+            pl.BlockSpec((1, rows + ranks, part), lambda i: (i, 0, 0)),
+            pl.BlockSpec((ranks, 1), lambda i: (0, 0)),
+        ],
+        out_specs=(pl.BlockSpec((rows, part), lambda i: (0, i)), pl.BlockSpec((ranks, part), lambda i: (0, i))),
+        compiler_params=pltpu.CompilerParams(vmem_limit_bytes=16 << 20),
+        cost_estimate=pl.CostEstimate(flops=2 * buffer.size, bytes_accessed=12 * buffer.size, transcendentals=0),
+    )(buffer, back, squares)
+
+
+def sums_kernel(nzh, nzl, left_ref, tall_ref, out_ref, gram_ref):
+    y_at = lax.axis_index("y")
+    ranks = left_ref.shape[1] // (nzh * nzl)
+    tiles = tall_ref.shape[1] // LANES
+    left = left_ref[...]
+    gram_ref[...] = dot(left, left, (0, 0))
+    w = dot(left, tall_ref[...], (0, 0))
+    half = ranks // 2
+    lanes = pl.ds(pl.multiple_of((y_at % 2) * LANES, LANES), LANES)
+    for zh in range(nzh):
+        for zl in range(nzl):
+            first = (zh * nzl + zl) * ranks
+            for t in range(tiles):
+                out_ref[zl * nzh + zh, t * ranks : (t + 1) * ranks, :] = w[
+                    first : first + ranks, t * LANES : (t + 1) * LANES
+                ]
+            piece = pl.ds(pl.multiple_of(first + (y_at // 2) * half, half), half)
+            out_ref[zl * nzh + zh, tiles * ranks :, :] = gram_ref[piece, lanes]
+
+
+def sums(left, tall, nzh, nzl):
+    rank, part = left.shape[1], tall.shape[1]
+    ranks = rank // (nzh * nzl)
+    rows = part // LANES * ranks + ranks // 2
     vmem = pl.BlockSpec(memory_space=pltpu.VMEM)
     return pl.pallas_call(
-        inverse_factor_kernel,
-        out_shape=jax.ShapeDtypeStruct(gram.shape, jnp.float32),
-        in_specs=[vmem],
+        functools.partial(sums_kernel, nzh, nzl),
+        out_shape=jax.ShapeDtypeStruct((nzl * nzh, rows, LANES), jnp.float32),
+        in_specs=[vmem, vmem],
         out_specs=vmem,
-        compiler_params=pltpu.CompilerParams(vmem_limit_bytes=16 << 20),
-        cost_estimate=pl.CostEstimate(flops=2 * 256**3, bytes_accessed=2 * 256 * 256 * 4, transcendentals=256),
-    )(gram)
+        scratch_shapes=[pltpu.VMEM((rank, rank), jnp.float32)],
+        compiler_params=pltpu.CompilerParams(vmem_limit_bytes=24 << 20),
+        cost_estimate=pl.CostEstimate(
+            flops=12 * left.shape[0] * rank * (part + rank), bytes_accessed=4 * left.size + 8 * tall.size, transcendentals=0
+        ),
+    )(left, tall)
+
+
+def finish_kernel(nx, gram_ref, left_ref, w_ref, back_ref, ortho_ref, squares_ref, inverse_ref, all_ref, right_ref):
+    x_at, z_at = lax.axis_index("x"), lax.axis_index(Z)
+    nz, slab, _ = w_ref.shape
+    rank = inverse_ref.shape[0]
+    ranks = rank // nz
+    rows = left_ref.shape[0] // nx
+    half = ranks // 2
+    x11, x21, x22 = inverse_factor(gram_ref[...])
+    inverse_ref[:HALF, :HALF] = x11
+    inverse_ref[:HALF, HALF:] = jnp.zeros((HALF, HALF), jnp.float32)
+    inverse_ref[HALF:, :HALF] = x21
+    inverse_ref[HALF:, HALF:] = x22
+    inverse = inverse_ref[...]
+    tiles = (slab - half) // ranks
+    for t in range(tiles):
+        w = jnp.concatenate([w_ref[z, t * ranks : (t + 1) * ranks, :] for z in range(nz)], axis=0)
+        right_ref[:, t * LANES : (t + 1) * LANES] = dot(inverse, w, (1, 0))
+    all_ref[...] = dot(left_ref[...], inverse, (1, 1))
+    ortho_ref[...] = all_ref[pl.ds(pl.multiple_of(x_at * rows, rows), rows), :]
+
+    right = right_ref[...]
+    right_high = right.astype(jnp.bfloat16)
+    right_low = (right - right_high.astype(jnp.float32)).astype(jnp.bfloat16)
+    for x in range(nx):
+        q = all_ref[x * rows : (x + 1) * rows, :]
+        q_high = q.astype(jnp.bfloat16)
+        q_low = (q - q_high.astype(jnp.float32)).astype(jnp.bfloat16)
+        plain = lax.Precision.DEFAULT
+        small = dot(q_low, right_high, (1, 0), plain) + dot(q_high, right_low, (1, 0), plain)
+        back_ref[x, :rows, :] = small + dot(q_high, right_high, (1, 0), plain)
+    mine = right_ref[pl.ds(pl.multiple_of(z_at * ranks, ranks), ranks), :]
+    each = ranks // nx
+    for x in range(nx):
+        back_ref[x, rows : rows + each, :] = mine[x * each : (x + 1) * each, :]
+    squares_ref[...] = jnp.broadcast_to(jnp.sum(mine * mine, axis=1, keepdims=True), squares_ref.shape)
+
+
+def finish(gram, left, w, nx):
+    rank = gram.shape[0]
+    nz, slab, _ = w.shape
+    ranks = rank // nz
+    rows = left.shape[0] // nx
+    part = (slab - ranks // 2) // ranks * LANES
+    vmem = pl.BlockSpec(memory_space=pltpu.VMEM)
+    return pl.pallas_call(
+        functools.partial(finish_kernel, nx),
+        out_shape=(
+            jax.ShapeDtypeStruct((nx, rows + ranks // nx, part), jnp.float32),
+            jax.ShapeDtypeStruct((rows, rank), jnp.float32),
+            jax.ShapeDtypeStruct((ranks, LANES), jnp.float32),
+        ),
+        in_specs=[vmem] * 3,
+        out_specs=(vmem, vmem, vmem),
+        scratch_shapes=[
+            pltpu.VMEM((rank, rank), jnp.float32),
+            pltpu.VMEM(left.shape, jnp.float32),
+            pltpu.VMEM((rank, part), jnp.float32),
+        ],
+        compiler_params=pltpu.CompilerParams(vmem_limit_bytes=32 << 20),
+        cost_estimate=pl.CostEstimate(
+            flops=12 * rank**3 + 6 * left.shape[0] * rank * part, bytes_accessed=8 * left.shape[0] * part, transcendentals=256
+        ),
+    )(gram, left, w)
 
 
 def on_device(momentum, gradient, basis):
     rows, columns = momentum.shape
     ranks = basis.shape[1]
     rank = 256
-    nx, ny = lax.axis_size("x"), lax.axis_size("y")
-    nzh, nzl = lax.axis_size("zh"), lax.axis_size("zl")
-    nz = nzh * nzl
+    nx, ny, nzh, nzl = lax.axis_size("x"), lax.axis_size("y"), lax.axis_size("zh"), lax.axis_size("zl")
     part = columns // nx
-    x_at, y_at = lax.axis_index("x"), lax.axis_index("y")
-
-    buffer = momentum + gradient.astype(jnp.float32)
-    tall = lax.all_to_all(buffer.reshape(rows, nx, part).transpose(1, 0, 2), "x", 0, 0, tiled=True)
-    tall = tall.reshape(nx * rows, part)
+    own_ranks = nx * ranks
+    peers = lax.axis_size(GROUP)
+
     v = lax.all_to_all(basis.T.reshape(ranks, nx, part).transpose(1, 0, 2), "x", 0, 0, tiled=True)
-    v = lax.all_gather(v.reshape(nx * ranks, part), Z, axis=0, tiled=True)
+    buffer = split(momentum, gradient, nx)
+    tall = lax.all_to_all(buffer, "x", 0, 0, tiled=True).reshape(nx * rows, part)
+    v = lax.all_gather(v.reshape(own_ranks, part), Z, axis=0, tiled=True)
 
     partial = dot(tall, v, (1, 1))
-    peers = lax.axis_size(GROUP)
     piece = partial.shape[0] // peers
     parts = lax.all_to_all(partial.reshape(peers, piece, rank), GROUP, 0, 0, tiled=True)
     own = jnp.sum(parts, axis=0)
     left = lax.all_to_all(jnp.broadcast_to(own[None], (peers, piece, rank)), GROUP, 0, 0, tiled=True)
     left = left.reshape(nx * rows, rank)
 
-    slab = rank // ny
-    w_part = dot(left, tall, (0, 0))
-    g_part = dot(left, lax.dynamic_slice_in_dim(left, y_at * slab, slab, 1), (0, 0))
-    both = jnp.concatenate([w_part, g_part], axis=1).reshape(nzh, nzl, rank // nz, part + slab)
-    both = jnp.sum(lax.all_to_all(both, "zl", 1, 1, tiled=True), axis=1)
+    both = sums(left, tall, nzh, nzl)
+    slab = both.shape[1]
+    both = lax.all_to_all(both, "zl", 0, 0, tiled=True)
+    both = jnp.sum(both.reshape(nzl, nzh, slab, LANES), axis=0)
     both = jnp.sum(lax.all_to_all(both, "zh", 0, 0, tiled=True), axis=0)
-    both = lax.all_gather(both, Z, axis=0, tiled=True)
-    w = both[:, :part]
-    gram = lax.all_gather(both[:, part:].T, "y", axis=0, tiled=True)
-    inverse = inverse_factor((gram + gram.T) * 0.5)
-
-    ortho = dot(left, inverse, (1, 1))
-    orthonormal = lax.dynamic_slice_in_dim(ortho, x_at * rows, rows, 0)
-    right = dot(inverse, w, (1, 0))
-
-    z_at = lax.axis_index(Z)
-    mine = lax.dynamic_slice_in_dim(right, z_at * (nx * ranks), nx * ranks, 0)
-    mine = lax.all_to_all(mine.reshape(nx, ranks, part), "x", 0, 0, tiled=True)
-    mine = mine.transpose(1, 0, 2).reshape(ranks, columns)
-    squares = lax.psum(jnp.sum(mine * mine, axis=1), ("y", "core"))
-    new_basis = (mine / (jnp.sqrt(squares) + column_eps)[:, None]).T
-
-    feedback = dot(ortho, right, (1, 0))
-    feedback = lax.all_to_all(feedback.reshape(nx, rows, part), "x", 0, 0, tiled=True)
-    feedback = feedback.transpose(1, 0, 2).reshape(rows, columns)
-    new_momentum = buffer - (1.0 - momentum_keep) * feedback
+    both = lax.all_gather(both, Z, axis=0)
+    half = own_ranks // 2
+    gram = both[:, slab - half :]
+    gram = lax.all_to_all(jnp.broadcast_to(gram[None], (ny, *gram.shape)), "y", 0, 0, tiled=True)
+    gram = gram.reshape(2, 2, nzh * nzl, half, LANES).transpose(2, 0, 3, 1, 4).reshape(rank, rank)
+
+    back, orthonormal, squares = finish(gram, left, both, nx)
+    squares = lax.psum(lax.psum(lax.psum(squares[:, 0], "core"), "y"), "x")
+    squares = lax.dynamic_slice_in_dim(squares, lax.axis_index("x") * ranks, ranks, 0)
+    back = lax.all_to_all(back, "x", 0, 0, tiled=True)
+    new_momentum, new_basis = join(buffer, back, squares[:, None])
+    new_basis = new_basis.T
     return (new_momentum, orthonormal, new_basis)
 
 

time: 246 us -> 235 us (0.955)
  blocking collectives: 155 us -> 191 us
  waiting for transfers between devices: 28.6 us -> 0.01 us
  starting transfers between devices: 25.5 us -> 12.7 us
  Pallas kernels: 14.2 us -> 22 us
  matrix products: 9.52 us -> 1.81 us
  other arithmetic: 5.32 us -> 0.12 us
    all_to_all x1 -> x4, blocking collectives: 28.4 us -> 71 us  [the longest x1 26.8 us: on_device(): both = lax.all_to_all(both, 'zl', 0, 0, tiled=True)]
    all_to_all x5 -> x2, waiting for transfers between devices: 28.6 us -> 0.01 us  [the longest x1 0.01 us: on_device(): lax.all_to_all(buffer, 'x', 0, 0, tiled=True).reshape(nx * rows, part)]
    all_to_all x5 -> x2, starting transfers between devices: 20.7 us -> 7.83 us  [the longest x1 4.24 us: on_device(): lax.all_to_all(buffer, 'x', 0, 0, tiled=True).reshape(nx * rows, part)]
    all_gather x3 -> x2, blocking collectives: 74 us -> 63.6 us  [the longest x1 34.9 us: on_device(): v = lax.all_gather(v.reshape(own_ranks, part), Z, axis=0, tiled=True)]
    pallas_call x1 -> x4, Pallas kernels: 14.2 us -> 22 us  [the longest x1 14 us: finish(): pl.pallas_call(functools.partial(finish_kernel, nx), out_shape=(jax.Shape...]
    dot_general x6 -> x1, matrix products: 9.52 us -> 1.81 us  [dot(): lax.dot_general(a, b, ((contract[:1], contract[1:]), ((), ())), precision...]
    psum x1 -> x3, blocking collectives: 25.5 us -> 29.2 us  [on_device(): squares = lax.psum(lax.psum(lax.psum(squares[:, 0], 'core'), 'y'), 'x')]
  transfers between devices with their start and end apart: 6 -> 3, of which waited for: 3 -> 0; matrix products, arithmetic and copies ran while one was open for 3% -> 0% of each run, Pallas kernels for 0% -> 1%
where the time goes in v2:
time: 235 us; the launch traced here: 232 us
  blocking collectives  191 us (81%)
  Pallas kernels  22 us (9%)
  starting transfers between devices  12.7 us (5%)
  local copies, waits for them, and re-layouts  4.35 us (2%)
    all_gather x1, blocking collectives, on_device(): v = lax.all_gather(v.reshape(own_ranks, part), Z, axis=0, tiled=True)  34.9 us
    psum x3, blocking collectives, on_device(): squares = lax.psum(lax.psum(lax.psum(squares[:, 0], 'core'), 'y'), 'x')  29.2 us
    all_gather x1, blocking collectives, on_device(): both = lax.all_gather(both, Z, axis=0)  28.8 us
    all_to_all x1, blocking collectives, on_device(): lax.all_to_all(partial.reshape(peers, piece, rank), GROUP, 0, 0, tiled=True)  26.9 us
    all_to_all x1, blocking collectives, on_device(): both = lax.all_to_all(both, 'zl', 0, 0, tiled=True)  26.8 us
    all_to_all x1, blocking collectives, on_device(): both = jnp.sum(lax.all_to_all(both, 'zh', 0, 0, tiled=True), axis=0)  21.2 us
    all_to_all x1, blocking collectives, on_device(): lax.all_to_all(jnp.broadcast_to(own[None], (peers, piece, rank)), GROUP,...  15 us
    pallas_call x1, Pallas kernels, finish(): pl.pallas_call(functools.partial(finish_kernel, nx), out_shape=(jax.Shape...  14 us
  transfers between devices with their start and end apart: 3, of which 0 were waited for; matrix products, arithmetic and copies ran while one was open for 0% of the time, Pallas kernels for 1%

profile of v2, /device:TPU:1, one launch (start us, length us, event | category | flops | bytes accessed | tf_op | source)
XLA Modules:
  0.0 232.4 jit_solution(3551955850479184323)
XLA Ops:
  0.6 4.9 %all-to-all-start.1 = ((f32[4,4,896]{2,1,0:T(4,128)}), f32[4,4,896]{2,1,0:T(4,128)S(1)}, u32[]{:S(2)}, u32[]{:S(2)}) async-start(f32[4,4,896]{2,1,0:T(4,128)} %bitcast.30), calls=%async_computation.1 | async-start | bytes 114688 | tf_op jit(solution)/shard_map/all_to_all | solution.py:258
  5.5 0.0 copy-start.1
  5.5 1.5 copy-done.1
  7.0 0.0 copy-start.2
  7.0 1.2 copy-done.2
  8.2 2.0 shard_map.58.buffer_ref
  10.1 0.0 all-to-all-done.1
  10.1 4.2 %all-to-all-start = ((f32[4,128,896]{2,1,0:T(8,128)}), f32[4,128,896]{2,1,0:T(8,128)S(1)}, u32[]{:S(2)}, u32[]{:S(2)}) async-start(f32[4,128,896]{2,1,0:T(8,128)} %shard_map.58.buffer_ref), calls=%async_computation | async-start | bytes 3670016 | tf_op jit(solution)/shard_map/all_to_all | solution.py:260
  14.4 34.9 %all_gather.9 = f32[256,896]{1,0:T(8,128)S(1)} all-gather(f32[16,896]{1,0:T(8,128)S(1)} %reshape.33), channel_id=1, replica_groups=mesh['zh'=4,'zl'=4,'x'=4,'y'=4,'core'=2] {'zh','zl'}, dimensions={0}, use_global_device_ids=true | all-gather | bytes 974848 | tf_op jit(solution)/shard_map/all_gather | solution.py:261
  49.3 0.0 all-to-all-done
  49.3 1.8 fusion
  51.1 26.9 %all_to_all.40 = f32[32,16,256]{2,1,0:T(8,128)S(1)} all-to-all(f32[32,16,256]{2,1,0:T(8,128)S(1)} %fusion), channel_id=1, replica_groups=mesh['zh'=4,'zl'=4,'x'=4,'y'=4,'core'=2] {'x','y','core'}, dimensions={0} | all-to-all | bytes 1048576 | tf_op jit(solution)/shard_map/all_to_all | solution.py:265
  78.1 0.1 broadcast_in_dim.6
  78.1 15.0 %all_to_all.41 = f32[32,16,256]{2,1,0:T(8,128)S(1)} all-to-all(f32[32,16,256]{2,1,0:T(8,128)S(1)} %broadcast_in_dim.6), channel_id=1, replica_groups=mesh['zh'=4,'zl'=4,'x'=4,'y'=4,'core'=2] {'x','y','core'}, dimensions={0} | all-to-all | bytes 1048576 | tf_op jit(solution)/shard_map/all_to_all | solution.py:267
  93.2 2.4 %shard_map.59 = f32[16,120,128]{2,1,0:T(8,128)S(1)} custom-call(f32[512,256]{1,0:T(8,128)S(1)} %bitcast.25, f32[512,896]{1,0:T(8,128)S(1)} %bitcast.22), custom_call_target="tpu_custom_call" | custom-call | flops 1811939328 | bytes 4194304 | tf_op jit(solution)/shard_map/pallas_call | solution.py:171
  95.5 26.8 %all_to_all.42 = f32[16,120,128]{2,1,0:T(8,128)S(1)} all-to-all(f32[16,120,128]{2,1,0:T(8,128)S(1)} %shard_map.59), channel_id=1, replica_groups=mesh['zh'=4,'zl'=4,'x'=4,'y'=4,'core'=2] {'zl'}, dimensions={0} | all-to-all | bytes 1966080 | tf_op jit(solution)/shard_map/all_to_all | solution.py:272
  122.4 0.1 reduce_sum.28
  122.4 21.2 %all_to_all.43 = f32[4,120,128]{2,1,0:T(8,128)S(1)} all-to-all(f32[4,120,128]{2,1,0:T(8,128)S(1)} %reduce_sum.28), channel_id=1, replica_groups=mesh['zh'=4,'zl'=4,'x'=4,'y'=4,'core'=2] {'zh'}, dimensions={0} | all-to-all | bytes 491520 | tf_op jit(solution)/shard_map/all_to_all | solution.py:274
  143.7 28.8 %all-gather = f32[1920,128]{1,0:T(8,128)S(1)} all-gather(f32[120,128]{1,0:T(8,128)S(1)} %reduce_sum.29), channel_id=2, replica_groups=mesh['zh'=4,'zl'=4,'x'=4,'y'=4,'core'=2] {'zh','zl'}, dimensions={0}, use_global_device_ids=true | all-gather | bytes 1044480 | tf_op jit(solution)/shard_map/all_gather | solution.py:275
  172.4 7.9 %all_to_all.44 = f32[4,16,8,128]{3,2,1,0:T(8,128)S(1)} all-to-all(f32[4,16,8,128]{3,2,1,0:T(8,128)S(1)} %broadcast_in_dim.7), channel_id=1, replica_groups=mesh['zh'=4,'zl'=4,'x'=4,'y'=4,'core'=2] {'y'}, dimensions={0} | all-to-all | bytes 524288 | tf_op jit(solution)/shard_map/all_to_all | solution.py:278
  180.4 14.0 %shard_map.60 = (f32[4,132,896]{2,1,0:T(8,128)S(1)}, f32[128,256]{1,0:T(8,128)}, f32[16,128]{1,0:T(8,128)S(1)}) custom-call(f32[256,256]{1,0:T(8,128)S(1)} %bitcast.27, f32[512,256]{1,0:T(8,128)S(1)} %bitcast.26, f32[16,120,128]{2,1,0:T(8,128)S(1)} %bitcast.24), custom_call_target="tpu_custom_call" | custom-call | flops 905969664 | bytes 3670016 | tf_op jit(solution)/shard_map/pallas_call | solution.py:228
  194.3 0.0 copy-start
  194.4 1.3 copy-done
  195.6 3.6 %all-to-all-start.7 = ((f32[4,132,896]{2,1,0:T(8,128)}), f32[4,132,896]{2,1,0:T(8,128)S(1)}, u32[]{:S(2)}, u32[]{:S(2)}) async-start(f32[4,132,896]{2,1,0:T(8,128)} %copy-done), calls=%async_computation.7 | async-start | bytes 3899392 | tf_op jit(solution)/shard_map/all_to_all | solution.py:284
  199.2 0.1 slice_reduce_fusion
  199.3 13.1 %psum.21 = f32[16]{0:T(128)S(1)} all-reduce(f32[16]{0:T(128)S(1)} %slice_reduce_fusion), channel_id=1, replica_groups=mesh['zh'=4,'zl'=4,'x'=4,'y'=4,'core'=2] {'core'}, use_global_device_ids=true, to_apply=%region_3.0 | all-reduce | flops 16 | bytes 128 | tf_op jit(solution)/shard_map/psum | solution.py:282
  212.5 7.4 %psum.22 = f32[16]{0:T(128)S(1)} all-reduce(f32[16]{0:T(128)S(1)} %psum.21), channel_id=1, replica_groups=mesh['zh'=4,'zl'=4,'x'=4,'y'=4,'core'=2] {'y'}, use_global_device_ids=true, to_apply=%region_4.0 | all-reduce | flops 16 | bytes 128 | tf_op jit(solution)/shard_map/psum | solution.py:282
  219.9 8.6 %psum.23 = f32[16]{0:T(128)S(1)} all-reduce(f32[16]{0:T(128)S(1)} %psum.22), channel_id=1, replica_groups=mesh['zh'=4,'zl'=4,'x'=4,'y'=4,'core'=2] {'x'}, use_global_device_ids=true, to_apply=%region_5.0 | all-reduce | flops 16 | bytes 128 | tf_op jit(solution)/shard_map/psum | solution.py:282
  228.5 0.1 dynamic-slice_bitcast_fusion
  228.6 0.1 copy.15.squares_ref
  228.7 0.0 all-to-all-done.7.back_ref
  228.7 3.7 %shard_map.61 = (f32[128,3584]{1,0:T(8,128)}, f32[4,3584]{1,0:T(4,128)}) custom-call(f32[4,128,896]{2,1,0:T(8,128)} %shard_map.58.buffer_ref, f32[4,132,896]{2,1,0:T(8,128)S(1)} %all-to-all-done.7.back_ref, f32[4,1]{1,0:T(4,128)S(1)} %copy.15.squares_ref), custom_call_target="tpu_custom_call" | custom-call | flops 917504 | bytes 5505024 | tf_op jit(solution)/shard_map/pallas_call | solution.py:128
  (6 shorter events, 0.1 us)
Async XLA Ops:
  0.6 9.5 %all-to-all-start.1 = ((f32[4,4,896]{2,1,0:T(4,128)}), f32[4,4,896]{2,1,0:T(4,128)S(1)}, u32[]{:S(2)}, u32[]{:S(2)}) async-start(f32[4,4,896]{2,1,0:T(4,128)} %bitcast.30), calls=%async_computation.1 | async-start | bytes 114688 | tf_op jit(solution)/shard_map/all_to_all | solution.py:258
  5.5 1.5 copy-start.1
  7.0 1.2 copy-start.2
  10.1 39.1 %all-to-all-start = ((f32[4,128,896]{2,1,0:T(8,128)}), f32[4,128,896]{2,1,0:T(8,128)S(1)}, u32[]{:S(2)}, u32[]{:S(2)}) async-start(f32[4,128,896]{2,1,0:T(8,128)} %shard_map.58.buffer_ref), calls=%async_computation | async-start | bytes 3670016 | tf_op jit(solution)/shard_map/all_to_all | solution.py:260
  194.3 1.3 copy-start
  195.6 33.1 %all-to-all-start.7 = ((f32[4,132,896]{2,1,0:T(8,128)}), f32[4,132,896]{2,1,0:T(8,128)S(1)}, u32[]{:S(2)}, u32[]{:S(2)}) async-start(f32[4,132,896]{2,1,0:T(8,128)} %copy-done), calls=%async_computation.7 | async-start | bytes 3899392 | tf_op jit(solution)/shard_map/all_to_all | solution.py:284

commit v3 on v2

--- a/solution.py
+++ b/solution.py
@@ -16,6 +16,8 @@
 GROUP = ("x", "y", "core")
 HALF = 128
 LANES = 128
+SHIFT = 2
+STEP = 8
 
 
 def dot(a, b, contract, precision=high):
@@ -29,57 +31,51 @@
     groups = [block[8 * g : 8 * g + 8, :] for g in range(n // 8)]
     lane = lax.broadcasted_iota(jnp.int32, (1, n), 1)
     row_in_group = lax.broadcasted_iota(jnp.int32, (8, n), 0)
-    for k in range(0, n, 4):
+    for k in range(0, n, STEP):
         first, at = k // 8, k % 8
-        inside = (lane >= k) & (lane < k + 4)
+        inside = (lane >= k) & (lane < k + STEP)
         cols = {
-            g: [jnp.broadcast_to(groups[g][:, k + j : k + j + 1], (8, n)) for j in range(4)]
+            g: [jnp.broadcast_to(groups[g][:, k + j : k + j + 1], (8, n)) for j in range(STEP)]
             for g in range(first, n // 8)
         }
-        a = [[cols[first][j][at + i : at + i + 1, :] for j in range(i + 1)] for i in range(4)]
-        low = [[None] * 4 for _ in range(4)]
-        inv = [[None] * 4 for _ in range(4)]
-        for j in range(4):
-            pivot = a[j][j]
-            for m in range(j):
-                pivot = pivot - low[j][m] * low[j][m]
-            r = lax.rsqrt(pivot)
-            inv[j][j] = r
-            for i in range(j + 1, 4):
-                value = a[i][j]
-                for m in range(j):
-                    value = value - low[i][m] * low[j][m]
-                low[i][j] = value * r
-        for j in range(4):
-            for i in range(j + 1, 4):
+        low = [[None] * STEP for _ in range(STEP)]
+        inv = [[None] * STEP for _ in range(STEP)]
+        a = [[cols[first][j][at + i : at + i + 1, :] for j in range(i + 1)] for i in range(STEP)]
+        for j in range(STEP):
+            inv[j][j] = lax.rsqrt(a[j][j])
+            for i in range(j + 1, STEP):
+                low[i][j] = a[i][j] * inv[j][j]
+            for i in range(j + 1, STEP):
+                for m in range(j + 1, i + 1):
+                    a[i][m] = a[i][m] - low[i][j] * low[m][j]
+        for j in range(STEP):
+            for i in range(j + 1, STEP):
                 value = low[i][j] * inv[j][j]
                 for m in range(j + 1, i):
                     value = value + low[i][m] * inv[m][j]
                 inv[i][j] = -(value * inv[i][i])
         rows = []
-        for i in range(4):
+        for i in range(STEP):
             unit = jnp.where(lane == k + i, 1.0, 0.0)
             rows.append(jnp.where(inside, unit, groups[first][at + i : at + i + 1, :]))
         new = []
-        for j in range(4):
+        for j in range(STEP):
             value = inv[j][0] * rows[0]
             for i in range(1, j + 1):
                 value = value + inv[j][i] * rows[i]
             new.append(value)
         for g in range(first, n // 8):
-            if g == first and at == 4:
+            if g == first and at + STEP == 8:
                 updated = groups[g]
             else:
                 updated = jnp.where(inside, 0.0, groups[g])
-                for j in range(4):
+                for j in range(STEP):
                     factor = inv[j][0] * cols[g][0]
                     for i in range(1, j + 1):
                         factor = factor + inv[j][i] * cols[g][i]
                     updated = updated - factor * new[j]
             if g == first:
-                if at == 4:
-                    updated = groups[g]
-                for j in range(4):
+                for j in range(STEP):
                     updated = jnp.where(row_in_group == at + j, new[j], updated)
             groups[g] = updated
     whole = jnp.concatenate(groups, axis=0)
@@ -117,34 +113,33 @@
 
 
 def join_kernel(buffer_ref, back_ref, squares_ref, momentum_ref, basis_ref):
-    rows = momentum_ref.shape[0]
-    momentum_ref[...] = buffer_ref[0] - (1.0 - momentum_keep) * back_ref[0, :rows, :]
-    basis_ref[...] = back_ref[0, rows:, :] / (jnp.sqrt(squares_ref[...]) + column_eps)
+    parts, rows, part = buffer_ref.shape
+    scale = 1.0 / (jnp.sqrt(squares_ref[...]) + column_eps)
+    for i in range(parts):
+        at = slice(i * part, (i + 1) * part)
+        momentum_ref[:, at] = buffer_ref[i] - (1.0 - momentum_keep) * back_ref[i, :rows, :]
+        basis_ref[:, at] = back_ref[i, rows:, :] * scale
 
 
 def join(buffer, back, squares):
     parts, rows, part = buffer.shape
     ranks = back.shape[1] - rows
+    vmem = pl.BlockSpec(memory_space=pltpu.VMEM)
     return pl.pallas_call(
         join_kernel,
-        grid=(parts,),
         out_shape=(
             jax.ShapeDtypeStruct((rows, parts * part), jnp.float32),
             jax.ShapeDtypeStruct((ranks, parts * part), jnp.float32),
         ),
-        in_specs=[
-            pl.BlockSpec((1, rows, part), lambda i: (i, 0, 0)),
-            pl.BlockSpec((1, rows + ranks, part), lambda i: (i, 0, 0)),
-            pl.BlockSpec((ranks, 1), lambda i: (0, 0)),
-        ],
-        out_specs=(pl.BlockSpec((rows, part), lambda i: (0, i)), pl.BlockSpec((ranks, part), lambda i: (0, i))),
+        in_specs=[vmem] * 3,
+        out_specs=(vmem, vmem),
         compiler_params=pltpu.CompilerParams(vmem_limit_bytes=16 << 20),
         cost_estimate=pl.CostEstimate(flops=2 * buffer.size, bytes_accessed=12 * buffer.size, transcendentals=0),
     )(buffer, back, squares)
 
 
 def sums_kernel(nzh, nzl, left_ref, tall_ref, out_ref, gram_ref):
-    y_at = lax.axis_index("y")
+    y_at, shift = lax.axis_index("y"), lax.axis_index("core") * SHIFT
     ranks = left_ref.shape[1] // (nzh * nzl)
     tiles = tall_ref.shape[1] // LANES
     left = left_ref[...]
@@ -152,15 +147,15 @@
     w = dot(left, tall_ref[...], (0, 0))
     half = ranks // 2
     lanes = pl.ds(pl.multiple_of((y_at % 2) * LANES, LANES), LANES)
-    for zh in range(nzh):
-        for zl in range(nzl):
-            first = (zh * nzl + zl) * ranks
-            for t in range(tiles):
-                out_ref[zl * nzh + zh, t * ranks : (t + 1) * ranks, :] = w[
-                    first : first + ranks, t * LANES : (t + 1) * LANES
-                ]
-            piece = pl.ds(pl.multiple_of(first + (y_at // 2) * half, half), half)
-            out_ref[zl * nzh + zh, tiles * ranks :, :] = gram_ref[piece, lanes]
+    for z in range(nzh * nzl):
+        line = (z + nzh * nzl - shift) % (nzh * nzl)
+        at = (line % nzl) * nzh + line // nzl
+        first = z * ranks
+        for t in range(tiles):
+            tile = w[first : first + ranks, t * LANES : (t + 1) * LANES]
+            out_ref[pl.ds(at, 1), t * ranks : (t + 1) * ranks, :] = tile[None]
+        piece = pl.ds(pl.multiple_of(first + (y_at // 2) * half, half), half)
+        out_ref[pl.ds(at, 1), tiles * ranks :, :] = gram_ref[piece, lanes][None]
 
 
 def sums(left, tall, nzh, nzl):
@@ -246,6 +241,16 @@
     )(gram, left, w)
 
 
+def z_groups(nzh, nzl, cores):
+    nz = nzh * nzl
+    near, far = [], []
+    for core in range(cores):
+        at = [[((zh * nzl + zl + SHIFT * core) % nz) * cores + core for zl in range(nzl)] for zh in range(nzh)]
+        near += at
+        far += [list(group) for group in zip(*at)]
+    return near, far
+
+
 def on_device(momentum, gradient, basis):
     rows, columns = momentum.shape
     ranks = basis.shape[1]
@@ -269,9 +274,11 @@
 
     both = sums(left, tall, nzh, nzl)
     slab = both.shape[1]
-    both = lax.all_to_all(both, "zl", 0, 0, tiled=True)
+    lines = (*Z, "core")
+    near, far = z_groups(nzh, nzl, lax.axis_size("core"))
+    both = lax.all_to_all(both, lines, 0, 0, tiled=True, axis_index_groups=near)
     both = jnp.sum(both.reshape(nzl, nzh, slab, LANES), axis=0)
-    both = jnp.sum(lax.all_to_all(both, "zh", 0, 0, tiled=True), axis=0)
+    both = jnp.sum(lax.all_to_all(both, lines, 0, 0, tiled=True, axis_index_groups=far), axis=0)
     both = lax.all_gather(both, Z, axis=0)
     half = own_ranks // 2
     gram = both[:, slab - half :]

time: 235 us -> 226 us (0.962)
  blocking collectives: 191 us -> 185 us
  Pallas kernels: 22 us -> 19.6 us
    all_to_all x2, blocking collectives: 48 us -> 43.3 us  [the longest x1 21.8 us: on_device(): lax.all_to_all(both, lines, 0, 0, tiled=True, axis_index_groups=far)]
    psum x3, blocking collectives: 29.2 us -> 25.5 us  [on_device(): squares = lax.psum(lax.psum(lax.psum(squares[:, 0], 'core'), 'y'), 'x')]
    all_gather x1, blocking collectives: 28.8 us -> 31.5 us  [on_device(): both = lax.all_gather(both, Z, axis=0)]
where the time goes in v3:
time: 226 us; the launch traced here: 224 us
  blocking collectives  185 us (82%)
  Pallas kernels  19.6 us (9%)
  starting transfers between devices  12.7 us (6%)
  local copies, waits for them, and re-layouts  4.35 us (2%)
    all_gather x1, blocking collectives, on_device(): v = lax.all_gather(v.reshape(own_ranks, part), Z, axis=0, tiled=True)  34.9 us
    all_gather x1, blocking collectives, on_device(): both = lax.all_gather(both, Z, axis=0)  31.5 us
    all_to_all x1, blocking collectives, on_device(): lax.all_to_all(partial.reshape(peers, piece, rank), GROUP, 0, 0, tiled=True)  26.9 us
    psum x3, blocking collectives, on_device(): squares = lax.psum(lax.psum(lax.psum(squares[:, 0], 'core'), 'y'), 'x')  25.5 us
    all_to_all x1, blocking collectives, on_device(): lax.all_to_all(both, lines, 0, 0, tiled=True, axis_index_groups=far)  21.8 us
    all_to_all x1, blocking collectives, on_device(): both = lax.all_to_all(both, lines, 0, 0, tiled=True, axis_index_groups=near)  21.4 us
    all_to_all x1, blocking collectives, on_device(): lax.all_to_all(jnp.broadcast_to(own[None], (peers, piece, rank)), GROUP,...  15 us
    pallas_call x1, Pallas kernels, finish(): pl.pallas_call(functools.partial(finish_kernel, nx), out_shape=(jax.Shape...  12.3 us
  transfers between devices with their start and end apart: 3, of which 0 were waited for; matrix products, arithmetic and copies ran while one was open for 0% of the time, Pallas kernels for 1%

profile of v3, /device:TPU:1, one launch (start us, length us, event | category | flops | bytes accessed | tf_op | source)
XLA Modules:
  0.0 224.3 jit_solution(92689202879714537)
XLA Ops:
  0.6 4.9 %all-to-all-start.1 = ((f32[4,4,896]{2,1,0:T(4,128)}), f32[4,4,896]{2,1,0:T(4,128)S(1)}, u32[]{:S(2)}, u32[]{:S(2)}) async-start(f32[4,4,896]{2,1,0:T(4,128)} %bitcast.30), calls=%async_computation.1 | async-start | bytes 114688 | tf_op jit(solution)/shard_map/all_to_all | solution.py:263
  5.5 0.0 copy-start.1
  5.5 1.5 copy-done.1
  7.0 0.0 copy-start.2
  7.0 1.2 copy-done.2
  8.2 2.0 shard_map.58.buffer_ref
  10.1 0.0 all-to-all-done.1
  10.1 4.2 %all-to-all-start = ((f32[4,128,896]{2,1,0:T(8,128)}), f32[4,128,896]{2,1,0:T(8,128)S(1)}, u32[]{:S(2)}, u32[]{:S(2)}) async-start(f32[4,128,896]{2,1,0:T(8,128)} %shard_map.58.buffer_ref), calls=%async_computation | async-start | bytes 3670016 | tf_op jit(solution)/shard_map/all_to_all | solution.py:265
  14.4 34.9 %all_gather.9 = f32[256,896]{1,0:T(8,128)S(1)} all-gather(f32[16,896]{1,0:T(8,128)S(1)} %reshape.33), channel_id=1, replica_groups=mesh['zh'=4,'zl'=4,'x'=4,'y'=4,'core'=2] {'zh','zl'}, dimensions={0}, use_global_device_ids=true | all-gather | bytes 974848 | tf_op jit(solution)/shard_map/all_gather | solution.py:266
  49.3 0.0 all-to-all-done
  49.3 1.8 fusion
  51.1 26.9 %all_to_all.40 = f32[32,16,256]{2,1,0:T(8,128)S(1)} all-to-all(f32[32,16,256]{2,1,0:T(8,128)S(1)} %fusion), channel_id=1, replica_groups=mesh['zh'=4,'zl'=4,'x'=4,'y'=4,'core'=2] {'x','y','core'}, dimensions={0} | all-to-all | bytes 1048576 | tf_op jit(solution)/shard_map/all_to_all | solution.py:270
  78.1 0.1 broadcast_in_dim.6
  78.1 15.0 %all_to_all.41 = f32[32,16,256]{2,1,0:T(8,128)S(1)} all-to-all(f32[32,16,256]{2,1,0:T(8,128)S(1)} %broadcast_in_dim.6), channel_id=1, replica_groups=mesh['zh'=4,'zl'=4,'x'=4,'y'=4,'core'=2] {'x','y','core'}, dimensions={0} | all-to-all | bytes 1048576 | tf_op jit(solution)/shard_map/all_to_all | solution.py:272
  93.2 2.4 %shard_map.59 = f32[16,120,128]{2,1,0:T(8,128)S(1)} custom-call(f32[512,256]{1,0:T(8,128)S(1)} %bitcast.25, f32[512,896]{1,0:T(8,128)S(1)} %bitcast.22), custom_call_target="tpu_custom_call" | custom-call | flops 1811939328 | bytes 4194304 | tf_op jit(solution)/shard_map/pallas_call | solution.py:166
  95.5 21.4 %all_to_all.42 = f32[16,120,128]{2,1,0:T(8,128)S(1)} all-to-all(f32[16,120,128]{2,1,0:T(8,128)S(1)} %shard_map.59), channel_id=1, replica_groups={{0,32,64,96},{128,160,192,224},{256,288,320,352},{384,416,448,480},{65,..., dimensions={0} | all-to-all | bytes 1966080 | tf_op jit(solution)/shard_map/all_to_all | solution.py:279
  117.0 0.1 reduce_sum.28
  117.0 21.8 %all_to_all.43 = f32[4,120,128]{2,1,0:T(8,128)S(1)} all-to-all(f32[4,120,128]{2,1,0:T(8,128)S(1)} %reduce_sum.28), channel_id=1, replica_groups={{0,128,256,384},{32,160,288,416},{64,192,320,448},{96,224,352,480},{65,..., dimensions={0} | all-to-all | bytes 491520 | tf_op jit(solution)/shard_map/all_to_all | solution.py:281
  138.9 31.5 %all-gather = f32[1920,128]{1,0:T(8,128)S(1)} all-gather(f32[120,128]{1,0:T(8,128)S(1)} %reduce_sum.29), channel_id=2, replica_groups=mesh['zh'=4,'zl'=4,'x'=4,'y'=4,'core'=2] {'zh','zl'}, dimensions={0}, use_global_device_ids=true | all-gather | bytes 1044480 | tf_op jit(solution)/shard_map/all_gather | solution.py:282
  170.4 7.9 %all_to_all.44 = f32[4,16,8,128]{3,2,1,0:T(8,128)S(1)} all-to-all(f32[4,16,8,128]{3,2,1,0:T(8,128)S(1)} %broadcast_in_dim.7), channel_id=1, replica_groups=mesh['zh'=4,'zl'=4,'x'=4,'y'=4,'core'=2] {'y'}, dimensions={0} | all-to-all | bytes 524288 | tf_op jit(solution)/shard_map/all_to_all | solution.py:285
  178.4 12.3 %shard_map.60 = (f32[4,132,896]{2,1,0:T(8,128)S(1)}, f32[128,256]{1,0:T(8,128)}, f32[16,128]{1,0:T(8,128)S(1)}) custom-call(f32[256,256]{1,0:T(8,128)S(1)} %bitcast.27, f32[512,256]{1,0:T(8,128)S(1)} %bitcast.26, f32[16,120,128]{2,1,0:T(8,128)S(1)} %bitcast.24), custom_call_target="tpu_custom_call" | custom-call | flops 905969664 | bytes 3670016 | tf_op jit(solution)/shard_map/pallas_call | solution.py:223
  190.6 0.0 copy-start
  190.7 1.3 copy-done
  191.9 3.6 %all-to-all-start.7 = ((f32[4,132,896]{2,1,0:T(8,128)}), f32[4,132,896]{2,1,0:T(8,128)S(1)}, u32[]{:S(2)}, u32[]{:S(2)}) async-start(f32[4,132,896]{2,1,0:T(8,128)} %copy-done), calls=%async_computation.7 | async-start | bytes 3899392 | tf_op jit(solution)/shard_map/all_to_all | solution.py:291
  195.5 0.1 slice_reduce_fusion
  195.6 8.5 %psum.21 = f32[16]{0:T(128)S(1)} all-reduce(f32[16]{0:T(128)S(1)} %slice_reduce_fusion), channel_id=1, replica_groups=mesh['zh'=4,'zl'=4,'x'=4,'y'=4,'core'=2] {'core'}, use_global_device_ids=true, to_apply=%region_3.0 | all-reduce | flops 16 | bytes 128 | tf_op jit(solution)/shard_map/psum | solution.py:289
  204.1 7.4 %psum.22 = f32[16]{0:T(128)S(1)} all-reduce(f32[16]{0:T(128)S(1)} %psum.21), channel_id=1, replica_groups=mesh['zh'=4,'zl'=4,'x'=4,'y'=4,'core'=2] {'y'}, use_global_device_ids=true, to_apply=%region_4.0 | all-reduce | flops 16 | bytes 128 | tf_op jit(solution)/shard_map/psum | solution.py:289
  211.5 9.6 %psum.23 = f32[16]{0:T(128)S(1)} all-reduce(f32[16]{0:T(128)S(1)} %psum.22), channel_id=1, replica_groups=mesh['zh'=4,'zl'=4,'x'=4,'y'=4,'core'=2] {'x'}, use_global_device_ids=true, to_apply=%region_5.0 | all-reduce | flops 16 | bytes 128 | tf_op jit(solution)/shard_map/psum | solution.py:289
  221.1 0.1 dynamic-slice_bitcast_fusion
  221.2 0.1 copy.15.squares_ref
  221.3 0.0 all-to-all-done.7.back_ref
  221.3 3.0 %shard_map.61 = (f32[128,3584]{1,0:T(8,128)}, f32[4,3584]{1,0:T(4,128)}) custom-call(f32[4,128,896]{2,1,0:T(8,128)} %shard_map.58.buffer_ref, f32[4,132,896]{2,1,0:T(8,128)S(1)} %all-to-all-done.7.back_ref, f32[4,1]{1,0:T(4,128)S(1)} %copy.15.squares_ref), custom_call_target="tpu_custom_call" | custom-call | flops 917504 | bytes 5505024 | tf_op jit(solution)/shard_map/pallas_call | solution.py:128
  (6 shorter events, 0.1 us)
Async XLA Ops:
  0.6 9.5 %all-to-all-start.1 = ((f32[4,4,896]{2,1,0:T(4,128)}), f32[4,4,896]{2,1,0:T(4,128)S(1)}, u32[]{:S(2)}, u32[]{:S(2)}) async-start(f32[4,4,896]{2,1,0:T(4,128)} %bitcast.30), calls=%async_computation.1 | async-start | bytes 114688 | tf_op jit(solution)/shard_map/all_to_all | solution.py:263
  5.5 1.5 copy-start.1
  7.0 1.2 copy-start.2
  10.1 39.1 %all-to-all-start = ((f32[4,128,896]{2,1,0:T(8,128)}), f32[4,128,896]{2,1,0:T(8,128)S(1)}, u32[]{:S(2)}, u32[]{:S(2)}) async-start(f32[4,128,896]{2,1,0:T(8,128)} %shard_map.58.buffer_ref), calls=%async_computation | async-start | bytes 3670016 | tf_op jit(solution)/shard_map/all_to_all | solution.py:265
  190.6 1.3 copy-start
  191.9 29.4 %all-to-all-start.7 = ((f32[4,132,896]{2,1,0:T(8,128)}), f32[4,132,896]{2,1,0:T(8,128)S(1)}, u32[]{:S(2)}, u32[]{:S(2)}) async-start(f32[4,132,896]{2,1,0:T(8,128)} %copy-done), calls=%async_computation.7 | async-start | bytes 3899392 | tf_op jit(solution)/shard_map/all_to_all | solution.py:291

commit v4 on v3

--- a/solution.py
+++ b/solution.py
@@ -15,6 +15,8 @@
 Z = ("zh", "zl")
 GROUP = ("x", "y", "core")
 HALF = 128
+QUARTER = 64
+REST = 7 * QUARTER // 4
 LANES = 128
 SHIFT = 2
 STEP = 8
@@ -84,15 +86,6 @@
     return jnp.where(rows_at >= cols_at, whole, 0.0)
 
 
-def inverse_factor(gram):
-    x11 = inverse_factor_block(gram[:HALF, :HALF])
-    u = dot(x11, gram[:HALF, HALF:], (1, 0))
-    rest = gram[HALF:, HALF:] - dot(u, u, (0, 0))
-    t = dot(u, x11, (0, 0))
-    x22 = inverse_factor_block(rest)
-    return x11, -dot(x22, t, (1, 0)), x22
-
-
 def split_kernel(momentum_ref, gradient_ref, out_ref):
     out_ref[0] = momentum_ref[...] + gradient_ref[...].astype(jnp.float32)
 
@@ -138,15 +131,20 @@
     )(buffer, back, squares)
 
 
-def sums_kernel(nzh, nzl, left_ref, tall_ref, out_ref, gram_ref):
-    y_at, shift = lax.axis_index("y"), lax.axis_index("core") * SHIFT
+def sums_kernel(nzh, nzl, left_ref, tall_ref, out_ref, gram_ref, rest_ref):
+    core_at = lax.axis_index("core")
+    shift = core_at * SHIFT
     ranks = left_ref.shape[1] // (nzh * nzl)
     tiles = tall_ref.shape[1] // LANES
     left = left_ref[...]
     gram_ref[...] = dot(left, left, (0, 0))
     w = dot(left, tall_ref[...], (0, 0))
-    half = ranks // 2
-    lanes = pl.ds(pl.multiple_of((y_at % 2) * LANES, LANES), LANES)
+    first_rows, rest_rows = HALF // (nzh * nzl), REST // (nzh * nzl)
+    rest_ref[:HALF, :] = gram_ref[:HALF, HALF:]
+    rest_ref[HALF : HALF + QUARTER, :] = gram_ref[HALF + QUARTER :, HALF:]
+    corner = gram_ref[HALF : HALF + QUARTER, HALF : HALF + QUARTER]
+    rest_ref[HALF + QUARTER :, :] = jnp.concatenate([corner[: QUARTER // 2], corner[QUARTER // 2 :]], axis=1)
+    rest = rest_ref[pl.ds(pl.multiple_of(core_at * REST, 8), REST), :]
     for z in range(nzh * nzl):
         line = (z + nzh * nzl - shift) % (nzh * nzl)
         at = (line % nzl) * nzh + line // nzl
@@ -154,21 +152,22 @@
         for t in range(tiles):
             tile = w[first : first + ranks, t * LANES : (t + 1) * LANES]
             out_ref[pl.ds(at, 1), t * ranks : (t + 1) * ranks, :] = tile[None]
-        piece = pl.ds(pl.multiple_of(first + (y_at // 2) * half, half), half)
-        out_ref[pl.ds(at, 1), tiles * ranks :, :] = gram_ref[piece, lanes][None]
+        end = tiles * ranks + first_rows
+        out_ref[pl.ds(at, 1), tiles * ranks : end, :] = gram_ref[z * first_rows : (z + 1) * first_rows, :HALF][None]
+        out_ref[pl.ds(at, 1), end:, :] = rest[z * rest_rows : (z + 1) * rest_rows][None]
 
 
 def sums(left, tall, nzh, nzl):
     rank, part = left.shape[1], tall.shape[1]
     ranks = rank // (nzh * nzl)
-    rows = part // LANES * ranks + ranks // 2
+    rows = part // LANES * ranks + (HALF + REST) // (nzh * nzl)
     vmem = pl.BlockSpec(memory_space=pltpu.VMEM)
     return pl.pallas_call(
         functools.partial(sums_kernel, nzh, nzl),
         out_shape=jax.ShapeDtypeStruct((nzl * nzh, rows, LANES), jnp.float32),
         in_specs=[vmem, vmem],
         out_specs=vmem,
-        scratch_shapes=[pltpu.VMEM((rank, rank), jnp.float32)],
+        scratch_shapes=[pltpu.VMEM((rank, rank), jnp.float32), pltpu.VMEM((2 * REST, LANES), jnp.float32)],
         compiler_params=pltpu.CompilerParams(vmem_limit_bytes=24 << 20),
         cost_estimate=pl.CostEstimate(
             flops=12 * left.shape[0] * rank * (part + rank), bytes_accessed=4 * left.size + 8 * tall.size, transcendentals=0
@@ -176,36 +175,61 @@
     )(left, tall)
 
 
-def finish_kernel(nx, gram_ref, left_ref, w_ref, back_ref, ortho_ref, squares_ref, inverse_ref, all_ref, right_ref):
+def product_in_parts(a, b):
+    a_high, b_high = a.astype(jnp.bfloat16), b.astype(jnp.bfloat16)
+    a_low = (a - a_high.astype(jnp.float32)).astype(jnp.bfloat16)
+    b_low = (b - b_high.astype(jnp.float32)).astype(jnp.bfloat16)
+    plain = lax.Precision.DEFAULT
+    small = dot(a_low, b_high, (1, 0), plain) + dot(a_high, b_low, (1, 0), plain)
+    return small + dot(a_high, b_high, (1, 0), plain)
+
+
+def w_rows(w_ref, first, tiles, ranks):
+    slabs = range(first // ranks, (first + HALF) // ranks)
+    parts = [jnp.concatenate([w_ref[z, t * ranks : (t + 1) * ranks, :] for z in slabs], axis=0) for t in range(tiles)]
+    return jnp.concatenate(parts, axis=1)
+
+
+def first_kernel(tiles, ranks, w_ref, left_ref, x11_ref, right_ref, ortho_ref):
+    rows = HALF // w_ref.shape[0]
+    block = jnp.concatenate(
+        [w_ref[z, tiles * ranks : tiles * ranks + rows, :] for z in range(w_ref.shape[0])], axis=0
+    )
+    x11 = inverse_factor_block(block)
+    x11_ref[...] = x11
+    right_ref[...] = dot(x11, w_rows(w_ref, 0, tiles, ranks), (1, 0))
+    ortho_ref[...] = dot(left_ref[:, :HALF], x11, (1, 1))
+
+
+def finish_kernel(
+    nx, tiles, ranks, mine_ref, other_ref, w_ref, left_ref, x11_ref, right_one_ref, ortho_one_ref, back_ref, ortho_ref, squares_ref, all_ref, right_ref
+):
     x_at, z_at = lax.axis_index("x"), lax.axis_index(Z)
-    nz, slab, _ = w_ref.shape
-    rank = inverse_ref.shape[0]
-    ranks = rank // nz
     rows = left_ref.shape[0] // nx
-    half = ranks // 2
-    x11, x21, x22 = inverse_factor(gram_ref[...])
-    inverse_ref[:HALF, :HALF] = x11
-    inverse_ref[:HALF, HALF:] = jnp.zeros((HALF, HALF), jnp.float32)
-    inverse_ref[HALF:, :HALF] = x21
-    inverse_ref[HALF:, HALF:] = x22
-    inverse = inverse_ref[...]
-    tiles = (slab - half) // ranks
-    for t in range(tiles):
-        w = jnp.concatenate([w_ref[z, t * ranks : (t + 1) * ranks, :] for z in range(nz)], axis=0)
-        right_ref[:, t * LANES : (t + 1) * LANES] = dot(inverse, w, (1, 0))
-    all_ref[...] = dot(left_ref[...], inverse, (1, 1))
+    x11 = x11_ref[...]
+    is_first = lax.axis_index("core") == 0
+    mine = jnp.concatenate([mine_ref[z] for z in range(mine_ref.shape[0])], axis=0)
+    other = jnp.concatenate([other_ref[z] for z in range(other_ref.shape[0])], axis=0)
+    rest = jnp.concatenate([jnp.where(is_first, mine, other), jnp.where(is_first, other, mine)], axis=0)
+    folded = rest[HALF + QUARTER :]
+    corner = jnp.concatenate([folded[:, :QUARTER], folded[:, QUARTER:]], axis=0)
+    upper = jnp.concatenate([corner, jnp.zeros((QUARTER, QUARTER), jnp.float32)], axis=1)
+    lower = jnp.concatenate([upper, rest[HALF : HALF + QUARTER]], axis=0)
+    right_upper = (lax.broadcasted_iota(jnp.int32, (HALF, HALF), 1) >= QUARTER) & (
+        lax.broadcasted_iota(jnp.int32, (HALF, HALF), 0) < QUARTER
+    )
+    u = dot(x11, rest[:HALF], (1, 0))
+    x22 = inverse_factor_block(jnp.where(right_upper, lower.T, lower) - dot(u, u, (0, 0)))
+    x21 = -dot(x22, dot(u, x11, (0, 0)), (1, 0))
+    right_ref[:HALF, :] = right_one_ref[...]
+    all_ref[:, :HALF] = ortho_one_ref[...]
+    right_ref[HALF:, :] = dot(x21, w_rows(w_ref, 0, tiles, ranks), (1, 0)) + dot(
+        x22, w_rows(w_ref, HALF, tiles, ranks), (1, 0)
+    )
+    all_ref[:, HALF:] = dot(left_ref[:, :HALF], x21, (1, 1)) + dot(left_ref[:, HALF:], x22, (1, 1))
+    for x in range(nx):
+        back_ref[x, :rows, :] = product_in_parts(all_ref[x * rows : (x + 1) * rows, :], right_ref[...])
     ortho_ref[...] = all_ref[pl.ds(pl.multiple_of(x_at * rows, rows), rows), :]
-
-    right = right_ref[...]
-    right_high = right.astype(jnp.bfloat16)
-    right_low = (right - right_high.astype(jnp.float32)).astype(jnp.bfloat16)
-    for x in range(nx):
-        q = all_ref[x * rows : (x + 1) * rows, :]
-        q_high = q.astype(jnp.bfloat16)
-        q_low = (q - q_high.astype(jnp.float32)).astype(jnp.bfloat16)
-        plain = lax.Precision.DEFAULT
-        small = dot(q_low, right_high, (1, 0), plain) + dot(q_high, right_low, (1, 0), plain)
-        back_ref[x, :rows, :] = small + dot(q_high, right_high, (1, 0), plain)
     mine = right_ref[pl.ds(pl.multiple_of(z_at * ranks, ranks), ranks), :]
     each = ranks // nx
     for x in range(nx):
@@ -213,32 +237,42 @@
     squares_ref[...] = jnp.broadcast_to(jnp.sum(mine * mine, axis=1, keepdims=True), squares_ref.shape)
 
 
-def finish(gram, left, w, nx):
-    rank = gram.shape[0]
-    nz, slab, _ = w.shape
-    ranks = rank // nz
-    rows = left.shape[0] // nx
-    part = (slab - ranks // 2) // ranks * LANES
+def first(w, left, tiles, ranks):
     vmem = pl.BlockSpec(memory_space=pltpu.VMEM)
-    return pl.pallas_call(
-        functools.partial(finish_kernel, nx),
+    part = tiles * LANES
+    return pl.pallas_call(
+        functools.partial(first_kernel, tiles, ranks),
+        out_shape=(
+            jax.ShapeDtypeStruct((HALF, HALF), jnp.float32),
+            jax.ShapeDtypeStruct((HALF, part), jnp.float32),
+            jax.ShapeDtypeStruct((left.shape[0], HALF), jnp.float32),
+        ),
+        in_specs=[vmem] * 2,
+        out_specs=(vmem,) * 3,
+        compiler_params=pltpu.CompilerParams(vmem_limit_bytes=16 << 20),
+        cost_estimate=pl.CostEstimate(flops=12 * HALF**2 * (part + left.shape[0]), bytes_accessed=8 * w.size, transcendentals=HALF),
+    )(w, left)
+
+
+def finish(mine, other, w, left, one, nx, tiles, ranks):
+    rank = left.shape[1]
+    rows, part = left.shape[0] // nx, tiles * LANES
+    vmem = pl.BlockSpec(memory_space=pltpu.VMEM)
+    return pl.pallas_call(
+        functools.partial(finish_kernel, nx, tiles, ranks),
         out_shape=(
             jax.ShapeDtypeStruct((nx, rows + ranks // nx, part), jnp.float32),
             jax.ShapeDtypeStruct((rows, rank), jnp.float32),
             jax.ShapeDtypeStruct((ranks, LANES), jnp.float32),
         ),
-        in_specs=[vmem] * 3,
-        out_specs=(vmem, vmem, vmem),
-        scratch_shapes=[
-            pltpu.VMEM((rank, rank), jnp.float32),
-            pltpu.VMEM(left.shape, jnp.float32),
-            pltpu.VMEM((rank, part), jnp.float32),
-        ],
+        in_specs=[vmem] * 7,
+        out_specs=(vmem,) * 3,
+        scratch_shapes=[pltpu.VMEM(left.shape, jnp.float32), pltpu.VMEM((rank, part), jnp.float32)],
         compiler_params=pltpu.CompilerParams(vmem_limit_bytes=32 << 20),
         cost_estimate=pl.CostEstimate(
-            flops=12 * rank**3 + 6 * left.shape[0] * rank * part, bytes_accessed=8 * left.shape[0] * part, transcendentals=256
-        ),
-    )(gram, left, w)
+            flops=12 * rank**3 + 6 * left.shape[0] * rank * part, bytes_accessed=8 * left.shape[0] * part, transcendentals=HALF
+        ),
+    )(mine, other, w, left, *one)
 
 
 def z_groups(nzh, nzl, cores):
@@ -255,7 +289,7 @@
     rows, columns = momentum.shape
     ranks = basis.shape[1]
     rank = 256
-    nx, ny, nzh, nzl = lax.axis_size("x"), lax.axis_size("y"), lax.axis_size("zh"), lax.axis_size("zl")
+    nx, nzh, nzl = lax.axis_size("x"), lax.axis_size("zh"), lax.axis_size("zl")
     part = columns // nx
     own_ranks = nx * ranks
     peers = lax.axis_size(GROUP)
@@ -280,12 +314,12 @@
     both = jnp.sum(both.reshape(nzl, nzh, slab, LANES), axis=0)
     both = jnp.sum(lax.all_to_all(both, lines, 0, 0, tiled=True, axis_index_groups=far), axis=0)
     both = lax.all_gather(both, Z, axis=0)
-    half = own_ranks // 2
-    gram = both[:, slab - half :]
-    gram = lax.all_to_all(jnp.broadcast_to(gram[None], (ny, *gram.shape)), "y", 0, 0, tiled=True)
-    gram = gram.reshape(2, 2, nzh * nzl, half, LANES).transpose(2, 0, 3, 1, 4).reshape(rank, rank)
-
-    back, orthonormal, squares = finish(gram, left, both, nx)
+    tiles = part // LANES
+    rest = both[:, slab - REST // (nzh * nzl) :]
+    other = lax.ppermute(rest, "core", [(0, 1), (1, 0)])
+    one = first(both, left, tiles, own_ranks)
+
+    back, orthonormal, squares = finish(rest, other, both, left, one, nx, tiles, own_ranks)
     squares = lax.psum(lax.psum(lax.psum(squares[:, 0], "core"), "y"), "x")
     squares = lax.dynamic_slice_in_dim(squares, lax.axis_index("x") * ranks, ranks, 0)
     back = lax.all_to_all(back, "x", 0, 0, tiled=True)

time: 226 us -> 228 us (level)
  starting transfers between devices: 12.7 us -> 20.5 us
  blocking collectives: 185 us -> 180 us
    all_to_all x1 -> x0, blocking collectives: 7.92 us -> none  [on_device(): lax.all_to_all(jnp.broadcast_to(gram[None], (ny, *gram.shape)), 'y', 0, 0...]
    ppermute x0 -> x1, starting transfers between devices: none -> 7.77 us  [on_device(): other = lax.ppermute(rest, 'core', [(0, 1), (1, 0)])]
    pallas_call x1 -> x2, Pallas kernels: 12.3 us -> 12.6 us  [the longest x1 7.68 us: finish(): pl.pallas_call(functools.partial(finish_kernel, nx, tiles, ranks), out_sh...]
  transfers between devices with their start and end apart: 3 -> 4, of which waited for: 0 -> 0; matrix products, arithmetic and copies ran while one was open for 0% -> 0% of each run, Pallas kernels for 1% -> 3%
where the time goes in v4:
time: 228 us; the launch traced here: 227 us
  blocking collectives  180 us (79%)
  starting transfers between devices  20.5 us (9%)
  Pallas kernels  19.9 us (9%)
  local copies, waits for them, and re-layouts  4.32 us (2%)
    all_gather x1, blocking collectives, on_device(): v = lax.all_gather(v.reshape(own_ranks, part), Z, axis=0, tiled=True)  34.9 us
    all_gather x1, blocking collectives, on_device(): both = lax.all_gather(both, Z, axis=0)  33 us
    all_to_all x1, blocking collectives, on_device(): lax.all_to_all(partial.reshape(peers, piece, rank), GROUP, 0, 0, tiled=True)  26.9 us
    psum x3, blocking collectives, on_device(): squares = lax.psum(lax.psum(lax.psum(squares[:, 0], 'core'), 'y'), 'x')  26.2 us
    all_to_all x1, blocking collectives, on_device(): both = lax.all_to_all(both, lines, 0, 0, tiled=True, axis_index_groups=near)  22.7 us
    all_to_all x1, blocking collectives, on_device(): lax.all_to_all(both, lines, 0, 0, tiled=True, axis_index_groups=far)  21.1 us
    all_to_all x1, blocking collectives, on_device(): lax.all_to_all(jnp.broadcast_to(own[None], (peers, piece, rank)), GROUP,...  15 us
    ppermute x1, starting transfers between devices, on_device(): other = lax.ppermute(rest, 'core', [(0, 1), (1, 0)])  7.77 us
  transfers between devices with their start and end apart: 4, of which 0 were waited for; matrix products, arithmetic and copies ran while one was open for 0% of the time, Pallas kernels for 3%

profile of v4, /device:TPU:1, one launch (start us, length us, event | category | flops | bytes accessed | tf_op | source)
XLA Modules:
  0.0 227.1 jit_solution(9899682364496517827)
XLA Ops:
  0.6 4.9 %all-to-all-start.1 = ((f32[4,4,896]{2,1,0:T(4,128)}), f32[4,4,896]{2,1,0:T(4,128)S(1)}, u32[]{:S(2)}, u32[]{:S(2)}) async-start(f32[4,4,896]{2,1,0:T(4,128)} %bitcast.24), calls=%async_computation.1 | async-start | bytes 114688 | tf_op jit(solution)/shard_map/all_to_all | solution.py:297
  5.5 0.0 copy-start.1
  5.5 1.5 copy-done.1
  7.0 0.0 copy-start.2
  7.0 1.2 copy-done.2
  8.2 2.0 shard_map.58.buffer_ref
  10.1 0.0 all-to-all-done.1
  10.1 4.2 %all-to-all-start = ((f32[4,128,896]{2,1,0:T(8,128)}), f32[4,128,896]{2,1,0:T(8,128)S(1)}, u32[]{:S(2)}, u32[]{:S(2)}) async-start(f32[4,128,896]{2,1,0:T(8,128)} %shard_map.58.buffer_ref), calls=%async_computation | async-start | bytes 3670016 | tf_op jit(solution)/shard_map/all_to_all | solution.py:299
  14.4 34.9 %all_gather.9 = f32[256,896]{1,0:T(8,128)S(1)} all-gather(f32[16,896]{1,0:T(8,128)S(1)} %reshape.26), channel_id=1, replica_groups=mesh['zh'=4,'zl'=4,'x'=4,'y'=4,'core'=2] {'zh','zl'}, dimensions={0}, use_global_device_ids=true | all-gather | bytes 974848 | tf_op jit(solution)/shard_map/all_gather | solution.py:300
  49.3 0.0 all-to-all-done
  49.3 1.8 fusion
  51.1 26.9 %all_to_all.35 = f32[32,16,256]{2,1,0:T(8,128)S(1)} all-to-all(f32[32,16,256]{2,1,0:T(8,128)S(1)} %fusion), channel_id=1, replica_groups=mesh['zh'=4,'zl'=4,'x'=4,'y'=4,'core'=2] {'x','y','core'}, dimensions={0} | all-to-all | bytes 1048576 | tf_op jit(solution)/shard_map/all_to_all | solution.py:304
  78.1 0.1 broadcast_in_dim.4
  78.1 15.0 %all_to_all.36 = f32[32,16,256]{2,1,0:T(8,128)S(1)} all-to-all(f32[32,16,256]{2,1,0:T(8,128)S(1)} %broadcast_in_dim.4), channel_id=1, replica_groups=mesh['zh'=4,'zl'=4,'x'=4,'y'=4,'core'=2] {'x','y','core'}, dimensions={0} | all-to-all | bytes 1048576 | tf_op jit(solution)/shard_map/all_to_all | solution.py:306
  93.2 2.4 %shard_map.59 = f32[16,127,128]{2,1,0:T(8,128)S(1)} custom-call(f32[512,256]{1,0:T(8,128)S(1)} %bitcast.19, f32[512,896]{1,0:T(8,128)S(1)} %bitcast.18), custom_call_target="tpu_custom_call" | custom-call | flops 1811939328 | bytes 4194304 | tf_op jit(solution)/shard_map/pallas_call | solution.py:165
  95.5 22.7 %all_to_all.37 = f32[16,127,128]{2,1,0:T(8,128)S(1)} all-to-all(f32[16,127,128]{2,1,0:T(8,128)S(1)} %shard_map.59), channel_id=1, replica_groups={{0,32,64,96},{128,160,192,224},{256,288,320,352},{384,416,448,480},{65,..., dimensions={0} | all-to-all | bytes 2080768 | tf_op jit(solution)/shard_map/all_to_all | solution.py:313
  118.2 0.1 reduce_sum.28
  118.3 21.1 %all_to_all.38 = f32[4,127,128]{2,1,0:T(8,128)S(1)} all-to-all(f32[4,127,128]{2,1,0:T(8,128)S(1)} %reduce_sum.28), channel_id=1, replica_groups={{0,128,256,384},{32,160,288,416},{64,192,320,448},{96,224,352,480},{65,..., dimensions={0} | all-to-all | bytes 520192 | tf_op jit(solution)/shard_map/all_to_all | solution.py:315
  139.4 33.0 %all-gather.1.w_ref = f32[16,127,128]{2,1,0:T(8,128)S(1)} all-gather(f32[1,127,128]{2,1,0:T(8,128)S(1)} %bitcast.23), channel_id=2, replica_groups=mesh['zh'=4,'zl'=4,'x'=4,'y'=4,'core'=2] {'zh','zl'}, dimensions={0}, use_global_device_ids=true | all-gather | bytes 1105408 | tf_op jit(solution)/shard_map/all_gather | solution.py:316
  172.4 7.8 %collective-permute-start = (f32[16,7,128]{2,1,0:T(8,128)S(1)}, f32[16,7,128]{2,1,0:T(8,128)S(1)}, u32[]{:S(2)}, u32[]{:S(2)}) collective-permute-start(f32[16,7,128]{2,1,0:T(8,128)S(1)} %slice.8.mine_ref), channel_id=1, source_target_pairs={{0,1},{1,0},{2,3},{3,2},{4,5},{5,4},{6,7},{7,6},{8,9},{9,8},{10,11... | collective-permute-start | bytes 172040 | tf_op jit(solution)/shard_map/ppermute | solution.py:319
  180.2 4.9 %shard_map.60 = (f32[128,128]{1,0:T(8,128)S(1)}, f32[128,896]{1,0:T(8,128)S(1)}, f32[512,128]{1,0:T(8,128)S(1)}) custom-call(f32[16,127,128]{2,1,0:T(8,128)S(1)} %all-gather.1.w_ref, f32[512,256]{1,0:T(8,128)S(1)} %bitcast.20), custom_call_target="tpu_custom_call" | custom-call | flops 276824064 | bytes 2080768 | tf_op jit(solution)/shard_map/pallas_call | solution.py:243
  185.1 0.0 collective-permute-done.other_ref
  185.1 7.7 %shard_map.61 = (f32[4,132,896]{2,1,0:T(8,128)S(1)}, f32[128,256]{1,0:T(8,128)}, f32[16,128]{1,0:T(8,128)S(1)}) custom-call(f32[16,7,128]{2,1,0:T(8,128)S(1)} %slice.8.mine_ref, f32[16,7,128]{2,1,0:T(8,128)S(1)} %collective-permute-done.other_ref, f32[16,127,128]{2,1,0:T(8,128)S(1)} %all-gather.1.w_ref, f32[512,256]{1,0:T(8,128)S(1)} %bitcast.21, ...), custom_call_target="tpu_custom_call" | custom-call | flops 905969664 | bytes 3670016 | tf_op jit(solution)/shard_map/pallas_call | solution.py:261
  192.8 0.0 copy-start
  192.8 1.3 copy-done
  194.1 3.6 %all-to-all-start.6 = ((f32[4,132,896]{2,1,0:T(8,128)}), f32[4,132,896]{2,1,0:T(8,128)S(1)}, u32[]{:S(2)}, u32[]{:S(2)}) async-start(f32[4,132,896]{2,1,0:T(8,128)} %copy-done), calls=%async_computation.6 | async-start | bytes 3899392 | tf_op jit(solution)/shard_map/all_to_all | solution.py:325
  197.7 0.1 slice_reduce_fusion
  197.8 2.5 %psum.21 = f32[16]{0:T(128)S(1)} all-reduce(f32[16]{0:T(128)S(1)} %slice_reduce_fusion), channel_id=1, replica_groups=mesh['zh'=4,'zl'=4,'x'=4,'y'=4,'core'=2] {'core'}, use_global_device_ids=true, to_apply=%region_3.0 | all-reduce | flops 16 | bytes 128 | tf_op jit(solution)/shard_map/psum | solution.py:323
  200.3 7.6 %psum.22 = f32[16]{0:T(128)S(1)} all-reduce(f32[16]{0:T(128)S(1)} %psum.21), channel_id=1, replica_groups=mesh['zh'=4,'zl'=4,'x'=4,'y'=4,'core'=2] {'y'}, use_global_device_ids=true, to_apply=%region_4.0 | all-reduce | flops 16 | bytes 128 | tf_op jit(solution)/shard_map/psum | solution.py:323
  207.8 16.1 %psum.23 = f32[16]{0:T(128)S(1)} all-reduce(f32[16]{0:T(128)S(1)} %psum.22), channel_id=1, replica_groups=mesh['zh'=4,'zl'=4,'x'=4,'y'=4,'core'=2] {'x'}, use_global_device_ids=true, to_apply=%region_5.0 | all-reduce | flops 16 | bytes 128 | tf_op jit(solution)/shard_map/psum | solution.py:323
  224.0 0.1 dynamic-slice_bitcast_fusion
  224.1 0.1 copy.16.squares_ref
  224.2 0.0 all-to-all-done.6.back_ref
  224.2 3.0 %shard_map.62 = (f32[128,3584]{1,0:T(8,128)}, f32[4,3584]{1,0:T(4,128)}) custom-call(f32[4,128,896]{2,1,0:T(8,128)} %shard_map.58.buffer_ref, f32[4,132,896]{2,1,0:T(8,128)S(1)} %all-to-all-done.6.back_ref, f32[4,1]{1,0:T(4,128)S(1)} %copy.16.squares_ref), custom_call_target="tpu_custom_call" | custom-call | flops 917504 | bytes 5505024 | tf_op jit(solution)/shard_map/pallas_call | solution.py:121
  (4 shorter events, 0.1 us)
Async XLA Ops:
  0.6 9.5 %all-to-all-start.1 = ((f32[4,4,896]{2,1,0:T(4,128)}), f32[4,4,896]{2,1,0:T(4,128)S(1)}, u32[]{:S(2)}, u32[]{:S(2)}) async-start(f32[4,4,896]{2,1,0:T(4,128)} %bitcast.24), calls=%async_computation.1 | async-start | bytes 114688 | tf_op jit(solution)/shard_map/all_to_all | solution.py:297
  5.5 1.5 copy-start.1
  7.0 1.2 copy-start.2
  10.1 39.1 %all-to-all-start = ((f32[4,128,896]{2,1,0:T(8,128)}), f32[4,128,896]{2,1,0:T(8,128)S(1)}, u32[]{:S(2)}, u32[]{:S(2)}) async-start(f32[4,128,896]{2,1,0:T(8,128)} %shard_map.58.buffer_ref), calls=%async_computation | async-start | bytes 3670016 | tf_op jit(solution)/shard_map/all_to_all | solution.py:299
  172.4 12.7 %collective-permute-start = (f32[16,7,128]{2,1,0:T(8,128)S(1)}, f32[16,7,128]{2,1,0:T(8,128)S(1)}, u32[]{:S(2)}, u32[]{:S(2)}) collective-permute-start(f32[16,7,128]{2,1,0:T(8,128)S(1)} %slice.8.mine_ref), channel_id=1, source_target_pairs={{0,1},{1,0},{2,3},{3,2},{4,5},{5,4},{6,7},{7,6},{8,9},{9,8},{10,11... | collective-permute-start | bytes 172040 | tf_op jit(solution)/shard_map/ppermute | solution.py:319
  192.8 1.3 copy-start
  194.1 30.1 %all-to-all-start.6 = ((f32[4,132,896]{2,1,0:T(8,128)}), f32[4,132,896]{2,1,0:T(8,128)S(1)}, u32[]{:S(2)}, u32[]{:S(2)}) async-start(f32[4,132,896]{2,1,0:T(8,128)} %copy-done), calls=%async_computation.6 | async-start | bytes 3899392 | tf_op jit(solution)/shard_map/all_to_all | solution.py:325

commit v5 on v3

--- a/solution.py
+++ b/solution.py
@@ -112,16 +112,15 @@
     )(momentum, gradient)
 
 
-def join_kernel(buffer_ref, back_ref, squares_ref, momentum_ref, basis_ref):
+def join_kernel(buffer_ref, back_ref, momentum_ref, basis_ref):
     parts, rows, part = buffer_ref.shape
-    scale = 1.0 / (jnp.sqrt(squares_ref[...]) + column_eps)
     for i in range(parts):
         at = slice(i * part, (i + 1) * part)
         momentum_ref[:, at] = buffer_ref[i] - (1.0 - momentum_keep) * back_ref[i, :rows, :]
-        basis_ref[:, at] = back_ref[i, rows:, :] * scale
-
-
-def join(buffer, back, squares):
+        basis_ref[:, at] = back_ref[i, rows:, :]
+
+
+def join(buffer, back):
     parts, rows, part = buffer.shape
     ranks = back.shape[1] - rows
     vmem = pl.BlockSpec(memory_space=pltpu.VMEM)
@@ -131,11 +130,11 @@
             jax.ShapeDtypeStruct((rows, parts * part), jnp.float32),
             jax.ShapeDtypeStruct((ranks, parts * part), jnp.float32),
         ),
-        in_specs=[vmem] * 3,
+        in_specs=[vmem] * 2,
         out_specs=(vmem, vmem),
         compiler_params=pltpu.CompilerParams(vmem_limit_bytes=16 << 20),
         cost_estimate=pl.CostEstimate(flops=2 * buffer.size, bytes_accessed=12 * buffer.size, transcendentals=0),
-    )(buffer, back, squares)
+    )(buffer, back)
 
 
 def sums_kernel(nzh, nzl, left_ref, tall_ref, out_ref, gram_ref):
@@ -286,11 +285,13 @@
     gram = gram.reshape(2, 2, nzh * nzl, half, LANES).transpose(2, 0, 3, 1, 4).reshape(rank, rank)
 
     back, orthonormal, squares = finish(gram, left, both, nx)
-    squares = lax.psum(lax.psum(lax.psum(squares[:, 0], "core"), "y"), "x")
+    squares = lax.psum(lax.psum(squares[:, 0], "core"), "y")
+    others = [lax.ppermute(squares, "x", [(i, (i + d) % nx) for i in range(nx)]) for d in range(1, nx)]
+    squares = sum(others, squares)
     squares = lax.dynamic_slice_in_dim(squares, lax.axis_index("x") * ranks, ranks, 0)
     back = lax.all_to_all(back, "x", 0, 0, tiled=True)
-    new_momentum, new_basis = join(buffer, back, squares[:, None])
-    new_basis = new_basis.T
+    new_momentum, mine = join(buffer, back)
+    new_basis = (mine / (jnp.sqrt(squares) + column_eps)[:, None]).T
     return (new_momentum, orthonormal, new_basis)
 
 

time: 226 us -> 230 us (1.018)
  starting transfers between devices: 12.7 us -> 23.1 us
  blocking collectives: 185 us -> 175 us
    ppermute x0 -> x3, starting transfers between devices: none -> 10.4 us  [on_device(): lax.ppermute(squares, 'x', [(i, (i + d) % nx) for i in range(nx)])]
    psum x3 -> x2, blocking collectives: 25.5 us -> 15.9 us  [on_device(): squares = lax.psum(lax.psum(squares[:, 0], 'core'), 'y')]
  transfers between devices with their start and end apart: 3 -> 6, of which waited for: 0 -> 1; matrix products, arithmetic and copies ran while one was open for 0% -> 0% of each run, Pallas kernels for 1% -> 1%
where the time goes in v5:
time: 230 us; the launch traced here: 227 us
  blocking collectives  175 us (76%)
  starting transfers between devices  23.1 us (10%)
  Pallas kernels  19.5 us (8%)
  local copies, waits for them, and re-layouts  4.18 us (2%)
    all_gather x1, blocking collectives, on_device(): v = lax.all_gather(v.reshape(own_ranks, part), Z, axis=0, tiled=True)  34.9 us
    all_gather x1, blocking collectives, on_device(): both = lax.all_gather(both, Z, axis=0)  31.5 us
    all_to_all x1, blocking collectives, on_device(): lax.all_to_all(partial.reshape(peers, piece, rank), GROUP, 0, 0, tiled=True)  26.9 us
    all_to_all x1, blocking collectives, on_device(): lax.all_to_all(both, lines, 0, 0, tiled=True, axis_index_groups=far)  21.8 us
    all_to_all x1, blocking collectives, on_device(): both = lax.all_to_all(both, lines, 0, 0, tiled=True, axis_index_groups=near)  21.4 us
    psum x2, blocking collectives, on_device(): squares = lax.psum(lax.psum(squares[:, 0], 'core'), 'y')  15.9 us
    all_to_all x1, blocking collectives, on_device(): lax.all_to_all(jnp.broadcast_to(own[None], (peers, piece, rank)), GROUP,...  15 us
    pallas_call x1, Pallas kernels, finish(): pl.pallas_call(functools.partial(finish_kernel, nx), out_shape=(jax.Shape...  12.3 us
  transfers between devices with their start and end apart: 6, of which 1 were waited for; matrix products, arithmetic and copies ran while one was open for 0% of the time, Pallas kernels for 1%

profile of v5, /device:TPU:1, one launch (start us, length us, event | category | flops | bytes accessed | tf_op | source)
XLA Modules:
  0.0 227.5 jit_solution(10610889389888404843)
XLA Ops:
  0.6 4.9 %all-to-all-start.1 = ((f32[4,4,896]{2,1,0:T(4,128)}), f32[4,4,896]{2,1,0:T(4,128)S(1)}, u32[]{:S(2)}, u32[]{:S(2)}) async-start(f32[4,4,896]{2,1,0:T(4,128)} %bitcast.29), calls=%async_computation.1 | async-start | bytes 114688 | tf_op jit(solution)/shard_map/all_to_all | solution.py:262
  5.5 0.0 copy-start.1
  5.5 1.5 copy-done.1
  7.0 0.0 copy-start.2
  7.0 1.2 copy-done.2
  8.2 2.0 shard_map.58.buffer_ref
  10.1 0.0 all-to-all-done.1
  10.1 4.2 %all-to-all-start = ((f32[4,128,896]{2,1,0:T(8,128)}), f32[4,128,896]{2,1,0:T(8,128)S(1)}, u32[]{:S(2)}, u32[]{:S(2)}) async-start(f32[4,128,896]{2,1,0:T(8,128)} %shard_map.58.buffer_ref), calls=%async_computation | async-start | bytes 3670016 | tf_op jit(solution)/shard_map/all_to_all | solution.py:264
  14.4 34.9 %all_gather.9 = f32[256,896]{1,0:T(8,128)S(1)} all-gather(f32[16,896]{1,0:T(8,128)S(1)} %reshape.34), channel_id=1, replica_groups=mesh['zh'=4,'zl'=4,'x'=4,'y'=4,'core'=2] {'zh','zl'}, dimensions={0}, use_global_device_ids=true | all-gather | bytes 974848 | tf_op jit(solution)/shard_map/all_gather | solution.py:265
  49.3 0.0 all-to-all-done
  49.3 1.8 fusion
  51.1 26.9 %all_to_all.40 = f32[32,16,256]{2,1,0:T(8,128)S(1)} all-to-all(f32[32,16,256]{2,1,0:T(8,128)S(1)} %fusion), channel_id=1, replica_groups=mesh['zh'=4,'zl'=4,'x'=4,'y'=4,'core'=2] {'x','y','core'}, dimensions={0} | all-to-all | bytes 1048576 | tf_op jit(solution)/shard_map/all_to_all | solution.py:269
  78.1 0.1 broadcast_in_dim.4
  78.1 15.0 %all_to_all.41 = f32[32,16,256]{2,1,0:T(8,128)S(1)} all-to-all(f32[32,16,256]{2,1,0:T(8,128)S(1)} %broadcast_in_dim.4), channel_id=1, replica_groups=mesh['zh'=4,'zl'=4,'x'=4,'y'=4,'core'=2] {'x','y','core'}, dimensions={0} | all-to-all | bytes 1048576 | tf_op jit(solution)/shard_map/all_to_all | solution.py:271
  93.2 2.4 %shard_map.59 = f32[16,120,128]{2,1,0:T(8,128)S(1)} custom-call(f32[512,256]{1,0:T(8,128)S(1)} %bitcast.24, f32[512,896]{1,0:T(8,128)S(1)} %bitcast.21), custom_call_target="tpu_custom_call" | custom-call | flops 1811939328 | bytes 4194304 | tf_op jit(solution)/shard_map/pallas_call | solution.py:165
  95.5 21.4 %all_to_all.42 = f32[16,120,128]{2,1,0:T(8,128)S(1)} all-to-all(f32[16,120,128]{2,1,0:T(8,128)S(1)} %shard_map.59), channel_id=1, replica_groups={{0,32,64,96},{128,160,192,224},{256,288,320,352},{384,416,448,480},{65,..., dimensions={0} | all-to-all | bytes 1966080 | tf_op jit(solution)/shard_map/all_to_all | solution.py:278
  117.0 0.1 reduce_sum.28
  117.0 21.8 %all_to_all.43 = f32[4,120,128]{2,1,0:T(8,128)S(1)} all-to-all(f32[4,120,128]{2,1,0:T(8,128)S(1)} %reduce_sum.28), channel_id=1, replica_groups={{0,128,256,384},{32,160,288,416},{64,192,320,448},{96,224,352,480},{65,..., dimensions={0} | all-to-all | bytes 491520 | tf_op jit(solution)/shard_map/all_to_all | solution.py:280
  138.9 31.5 %all-gather = f32[1920,128]{1,0:T(8,128)S(1)} all-gather(f32[120,128]{1,0:T(8,128)S(1)} %reduce_sum.29), channel_id=2, replica_groups=mesh['zh'=4,'zl'=4,'x'=4,'y'=4,'core'=2] {'zh','zl'}, dimensions={0}, use_global_device_ids=true | all-gather | bytes 1044480 | tf_op jit(solution)/shard_map/all_gather | solution.py:281
  170.4 7.9 %all_to_all.44 = f32[4,16,8,128]{3,2,1,0:T(8,128)S(1)} all-to-all(f32[4,16,8,128]{3,2,1,0:T(8,128)S(1)} %broadcast_in_dim.5), channel_id=1, replica_groups=mesh['zh'=4,'zl'=4,'x'=4,'y'=4,'core'=2] {'y'}, dimensions={0} | all-to-all | bytes 524288 | tf_op jit(solution)/shard_map/all_to_all | solution.py:284
  178.4 12.3 %shard_map.60 = (f32[4,132,896]{2,1,0:T(8,128)S(1)}, f32[128,256]{1,0:T(8,128)}, f32[16,128]{1,0:T(8,128)S(1)}) custom-call(f32[256,256]{1,0:T(8,128)S(1)} %bitcast.26, f32[512,256]{1,0:T(8,128)S(1)} %bitcast.25, f32[16,120,128]{2,1,0:T(8,128)S(1)} %bitcast.23), custom_call_target="tpu_custom_call" | custom-call | flops 905969664 | bytes 3670016 | tf_op jit(solution)/shard_map/pallas_call | solution.py:222
  190.6 0.0 copy-start
  190.7 1.3 copy-done
  191.9 3.6 %all-to-all-start.7 = ((f32[4,132,896]{2,1,0:T(8,128)}), f32[4,132,896]{2,1,0:T(8,128)S(1)}, u32[]{:S(2)}, u32[]{:S(2)}) async-start(f32[4,132,896]{2,1,0:T(8,128)} %copy-done), calls=%async_computation.7 | async-start | bytes 3899392 | tf_op jit(solution)/shard_map/all_to_all | solution.py:292
  195.5 0.1 slice_reduce_fusion
  195.6 8.5 %psum.14 = f32[16]{0:T(128)S(1)} all-reduce(f32[16]{0:T(128)S(1)} %slice_reduce_fusion), channel_id=1, replica_groups=mesh['zh'=4,'zl'=4,'x'=4,'y'=4,'core'=2] {'core'}, use_global_device_ids=true, to_apply=%region_3.0 | all-reduce | flops 16 | bytes 128 | tf_op jit(solution)/shard_map/psum | solution.py:288
  204.1 7.4 %psum.15 = f32[16]{0:T(128)S(1)} all-reduce(f32[16]{0:T(128)S(1)} %psum.14), channel_id=1, replica_groups=mesh['zh'=4,'zl'=4,'x'=4,'y'=4,'core'=2] {'y'}, use_global_device_ids=true, to_apply=%region_4.0 | all-reduce | flops 16 | bytes 128 | tf_op jit(solution)/shard_map/psum | solution.py:288
  211.5 3.0 %collective-permute-start = (f32[16]{0:T(128)S(1)}, f32[16]{0:T(128)S(1)}, u32[]{:S(2)}, u32[]{:S(2)}) collective-permute-start(f32[16]{0:T(128)S(1)} %psum.15), channel_id=1, source_target_pairs={{0,8},{8,16},{16,24},{24,0},{1,9},{9,17},{17,25},{25,1},{2,10},{10... | collective-permute-start | bytes 200 | tf_op jit(solution)/shard_map/ppermute | solution.py:289
  214.6 4.9 %collective-permute-start.1 = (f32[16]{0:T(128)S(1)}, f32[16]{0:T(128)S(1)}, u32[]{:S(2)}, u32[]{:S(2)}) collective-permute-start(f32[16]{0:T(128)S(1)} %psum.15), channel_id=1, source_target_pairs={{0,16},{8,24},{16,0},{24,8},{1,17},{9,25},{17,1},{25,9},{2,18},{10... | collective-permute-start | bytes 200 | tf_op jit(solution)/shard_map/ppermute | solution.py:289
  219.5 2.5 %collective-permute-start.2 = (f32[16]{0:T(128)S(1)}, f32[16]{0:T(128)S(1)}, u32[]{:S(2)}, u32[]{:S(2)}) collective-permute-start(f32[16]{0:T(128)S(1)} %psum.15), channel_id=1, source_target_pairs={{0,24},{8,0},{16,8},{24,16},{1,25},{9,1},{17,9},{25,17},{2,26},{10... | collective-permute-start | bytes 200 | tf_op jit(solution)/shard_map/ppermute | solution.py:289
  222.0 0.0 collective-permute-done
  222.0 0.0 collective-permute-done.1
  222.0 1.8 collective-permute-done.2
  223.8 0.1 sqrt_add_fusion
  223.8 0.0 all-to-all-done.7.back_ref
  223.8 2.9 %shard_map.61 = (f32[128,3584]{1,0:T(8,128)}, f32[4,3584]{1,0:T(4,128)S(1)}) custom-call(f32[4,128,896]{2,1,0:T(8,128)} %shard_map.58.buffer_ref, f32[4,132,896]{2,1,0:T(8,128)S(1)} %all-to-all-done.7.back_ref), custom_call_target="tpu_custom_call" | custom-call | flops 917504 | bytes 5505024 | tf_op jit(solution)/shard_map/pallas_call | solution.py:127
  226.8 0.7 divide_bitcast_fusion
  (7 shorter events, 0.1 us)
Async XLA Ops:
  0.6 9.5 %all-to-all-start.1 = ((f32[4,4,896]{2,1,0:T(4,128)}), f32[4,4,896]{2,1,0:T(4,128)S(1)}, u32[]{:S(2)}, u32[]{:S(2)}) async-start(f32[4,4,896]{2,1,0:T(4,128)} %bitcast.29), calls=%async_computation.1 | async-start | bytes 114688 | tf_op jit(solution)/shard_map/all_to_all | solution.py:262
  5.5 1.5 copy-start.1
  7.0 1.2 copy-start.2
  10.1 39.1 %all-to-all-start = ((f32[4,128,896]{2,1,0:T(8,128)}), f32[4,128,896]{2,1,0:T(8,128)S(1)}, u32[]{:S(2)}, u32[]{:S(2)}) async-start(f32[4,128,896]{2,1,0:T(8,128)} %shard_map.58.buffer_ref), calls=%async_computation | async-start | bytes 3670016 | tf_op jit(solution)/shard_map/all_to_all | solution.py:264
  190.6 1.3 copy-start
  191.9 31.9 %all-to-all-start.7 = ((f32[4,132,896]{2,1,0:T(8,128)}), f32[4,132,896]{2,1,0:T(8,128)S(1)}, u32[]{:S(2)}, u32[]{:S(2)}) async-start(f32[4,132,896]{2,1,0:T(8,128)} %copy-done), calls=%async_computation.7 | async-start | bytes 3899392 | tf_op jit(solution)/shard_map/all_to_all | solution.py:292
  211.5 10.4 %collective-permute-start = (f32[16]{0:T(128)S(1)}, f32[16]{0:T(128)S(1)}, u32[]{:S(2)}, u32[]{:S(2)}) collective-permute-start(f32[16]{0:T(128)S(1)} %psum.15), channel_id=1, source_target_pairs={{0,8},{8,16},{16,24},{24,0},{1,9},{9,17},{17,25},{25,1},{2,10},{10... | collective-permute-start | bytes 200 | tf_op jit(solution)/shard_map/ppermute | solution.py:289
  214.6 7.4 %collective-permute-start.1 = (f32[16]{0:T(128)S(1)}, f32[16]{0:T(128)S(1)}, u32[]{:S(2)}, u32[]{:S(2)}) collective-permute-start(f32[16]{0:T(128)S(1)} %psum.15), channel_id=1, source_target_pairs={{0,16},{8,24},{16,0},{24,8},{1,17},{9,25},{17,1},{25,9},{2,18},{10... | collective-permute-start | bytes 200 | tf_op jit(solution)/shard_map/ppermute | solution.py:289
  219.5 4.3 %collective-permute-start.2 = (f32[16]{0:T(128)S(1)}, f32[16]{0:T(128)S(1)}, u32[]{:S(2)}, u32[]{:S(2)}) collective-permute-start(f32[16]{0:T(128)S(1)} %psum.15), channel_id=1, source_target_pairs={{0,24},{8,0},{16,8},{24,16},{1,25},{9,1},{17,9},{25,17},{2,26},{10... | collective-permute-start | bytes 200 | tf_op jit(solution)/shard_map/ppermute | solution.py:289
